TPU v7x, 256 devices: a whole 4x4x8 slice. The times are simulated.
256 devices in a mesh: col: 8 (over y_hi, x), dp: 32 (over z, y_lo, core).
Axes of the slice: x: 4, y: 4 (y_hi: 2, y_lo: 2; y = y_hi * 2 + y_lo), z: 8, core: 2. Of those that a mesh axis runs over, the one named last changes fastest.
Arguments:
- stem_input: bfloat16 [4, 8192, 256], P(None, 'dp'), may hold values from -6 to 6
- top_lower: float32 [4, 8192, 256], P(None, 'dp'), may hold values from -6 to 6
- top_upper: float32 [4, 2048, 512], P(None, 'dp'), may hold values from -6 to 6
- seed_lower: bfloat16 [4, 8192, 256], P(None, 'dp'), may hold values from -6 to 6
- seed_upper: bfloat16 [4, 2048, 512], P(None, 'dp'), may hold values from -6 to 6
- gamma_lower: float32 [8, 256], P('col'), may hold values from 0.7 to 1.3
- gamma_upper: float32 [8, 512], P('col'), may hold values from 0.7 to 1.3
- lift_weight: bfloat16 [8, 512, 256], P('col'), may hold values from -0.25 to 0.25
- inner_weight: bfloat16 [8, 256, 1024], P('col'), may hold values from -0.375 to 0.375
- outer_weight: bfloat16 [8, 1024, 256], P('col'), may hold values from -0.1875 to 0.1875
- merge_weight: bfloat16 [8, 1024, 512], P('col'), may hold values from -0.1875 to 0.1875
- expand_weight: bfloat16 [8, 512, 2048], P('col'), may hold values from -0.25 to 0.25
- reduce_weight: bfloat16 [8, 2048, 512], P('col'), may hold values from -0.125 to 0.125
Outputs:
- lift_grad: float32 [8, 512, 256], P('col', 'dp')
- inner_grad: float32 [8, 256, 1024], P('col', 'dp')
- outer_grad: float32 [8, 1024, 256], P('col', 'dp')
- merge_grad: float32 [8, 1024, 512], P('col', 'dp')
- expand_grad: float32 [8, 512, 2048], P('col', 'dp')
- reduce_grad: float32 [8, 2048, 512], P('col', 'dp')
- stem_grad: float32 [4, 8192, 256], P(None, 'dp')
All inputs are finite; a program needn't handle non-finite values.
Results may differ from a plain program's by a relative error of at most 0.027.
Values sent between devices are 32-bit elements; how exact they have to be, the bound alone decides.
A program may use at most 128 MiB of HBM per device.

v0:
```python
import math

import jax
import jax.numpy as jnp
from jax import lax
from jax.sharding import PartitionSpec as P


def shifted(array, axis, by):
    devices = lax.axis_size(axis)
    pairs = [(i, i + by) for i in range(devices) if 0 <= i + by < devices]
    return lax.ppermute(array, axis, pairs)


def normalize(values):
    return values * lax.rsqrt(jnp.mean(values * values, axis=-1, keepdims=True) + 1e-06)


def norm_back(values, cotangent):
    inverse = lax.rsqrt(jnp.mean(values * values, axis=-1, keepdims=True) + 1e-06)
    normed = values * inverse
    return inverse * (cotangent - normed * jnp.mean(cotangent * normed, axis=-1, keepdims=True))


def silu_back(hidden, cotangent):
    gate_value = jax.nn.sigmoid(hidden)
    return cotangent * gate_value * (1.0 + hidden * (1.0 - gate_value))


def product(left_side, right_side):
    return jnp.dot(left_side, right_side, preferred_element_type=jnp.float32)


def left_outer(left_side, right_side):
    return lax.dot_general(
        left_side, right_side, (((0,), (0,)), ((), ())), preferred_element_type=jnp.float32
    )


def right_outer(left_side, right_side):
    return lax.dot_general(
        left_side, right_side, (((1,), (1,)), ((), ())), preferred_element_type=jnp.float32
    )


def upper_forward(lower_cur, merge_w, expand_w, reduce_w):
    folded = lower_cur.reshape(-1, 4 * lower_cur.shape[1])
    folded_cast = normalize(folded).astype(jnp.bfloat16)
    merged = product(folded_cast, merge_w)
    merged_cast = normalize(merged).astype(jnp.bfloat16)
    hidden = product(merged_cast, expand_w)
    gated_cast = jax.nn.silu(hidden).astype(jnp.bfloat16)
    result = merged + product(gated_cast, reduce_w)
    return (result, (folded, folded_cast, merged, merged_cast, hidden, gated_cast))


def upper_backward(kept_values, cotangent, merge_w, expand_w, reduce_w):
    folded, folded_cast, merged, merged_cast, hidden, gated_cast = kept_values
    grad_cast = cotangent.astype(jnp.bfloat16)
    d_reduce = left_outer(gated_cast, grad_cast)
    hidden_cast = silu_back(hidden, right_outer(grad_cast, reduce_w)).astype(jnp.bfloat16)
    d_expand = left_outer(merged_cast, hidden_cast)
    merged_grad = (cotangent + norm_back(merged, right_outer(hidden_cast, expand_w))).astype(
        jnp.bfloat16
    )
    d_merge = left_outer(folded_cast, merged_grad)
    d_folded = norm_back(folded, right_outer(merged_grad, merge_w))
    return (d_folded.reshape(-1, d_folded.shape[1] // 4), (d_merge, d_expand, d_reduce))


def lower_forward(stem, upper_prev, lift_w, inner_w, outer_w):
    upper_cast = upper_prev.astype(jnp.bfloat16)
    lifted = product(upper_cast, lift_w)
    row_count = lifted.shape[0]
    spread = jnp.broadcast_to(lifted[:, None, :], (row_count, 4, lifted.shape[1])).reshape(
        row_count * 4, lifted.shape[1]
    )
    mixed_sum = stem.astype(jnp.float32) + spread
    normed_cast = normalize(mixed_sum).astype(jnp.bfloat16)
    hidden = product(normed_cast, inner_w)
    gated_cast = jax.nn.silu(hidden).astype(jnp.bfloat16)
    result = product(gated_cast, outer_w)
    return (result, (upper_cast, mixed_sum, normed_cast, hidden, gated_cast))


def lower_backward(kept_values, cotangent, lift_w, inner_w, outer_w):
    upper_cast, mixed_sum, normed_cast, hidden, gated_cast = kept_values
    grad_cast = cotangent.astype(jnp.bfloat16)
    d_outer = left_outer(gated_cast, grad_cast)
    hidden_cast = silu_back(hidden, right_outer(grad_cast, outer_w)).astype(jnp.bfloat16)
    d_inner = left_outer(normed_cast, hidden_cast)
    d_mixed = norm_back(mixed_sum, right_outer(hidden_cast, inner_w))
    row_count = upper_cast.shape[0]
    lifted_cast = d_mixed.reshape(row_count, 4, d_mixed.shape[1]).sum(axis=1).astype(jnp.bfloat16)
    d_lift = left_outer(upper_cast, lifted_cast)
    d_upper = right_outer(lifted_cast, lift_w)
    return (d_mixed, d_upper, (d_lift, d_inner, d_outer))


def column_step(
    stem, lower_cur, upper_cur, grad_lower, grad_upper, gain_lower, gain_upper, weights
):
    lift_w, inner_w, outer_w, merge_w, expand_w, reduce_w = weights
    upper_branch, kept_upper = upper_forward(lower_cur, merge_w, expand_w, reduce_w)
    upper_prev = (upper_cur - upper_branch) / gain_upper
    lower_branch, kept_lower = lower_forward(stem, upper_prev, lift_w, inner_w, outer_w)
    lower_prev = (lower_cur - lower_branch) / gain_lower
    from_upper, upper_grads = upper_backward(kept_upper, grad_upper, merge_w, expand_w, reduce_w)
    total_lower = grad_lower + from_upper
    d_stem, d_upper, lower_grads = lower_backward(kept_lower, total_lower, lift_w, inner_w, outer_w)
    grad_upper_prev = gain_upper * grad_upper + d_upper
    grad_lower_prev = gain_lower * total_lower
    grads = (
        lower_grads[0],
        lower_grads[1],
        lower_grads[2],
        upper_grads[0],
        upper_grads[1],
        upper_grads[2],
    )
    return (lower_prev, upper_prev, grad_lower_prev, grad_upper_prev, grads, d_stem)


def shards(
    stem_input,
    top_lower,
    top_upper,
    seed_lower,
    seed_upper,
    gamma_lower,
    gamma_upper,
    lift_weight,
    inner_weight,
    outer_weight,
    merge_weight,
    expand_weight,
    reduce_weight,
):
    batches = stem_input.shape[0]
    rows_lower = stem_input.shape[1]
    channels = stem_input.shape[2]
    rows_upper = top_upper.shape[1]
    width_upper = top_upper.shape[2]
    pieces = 1
    total_pieces = batches * pieces
    piece_lower = rows_lower // pieces
    piece_upper = rows_upper // pieces
    weights = (
        lift_weight[0],
        inner_weight[0],
        outer_weight[0],
        merge_weight[0],
        expand_weight[0],
        reduce_weight[0],
    )
    gain_lower = gamma_lower[0]
    gain_upper = gamma_upper[0]
    groups = lax.axis_size("col")
    column_index = lax.axis_index("col")
    is_last = column_index == groups - 1

    def column_work(operands):
        stem, lower_cur, upper_cur, grad_low, grad_up = operands
        return column_step(
            stem, lower_cur, upper_cur, grad_low, grad_up, gain_lower, gain_upper, weights
        )

    def skipped(operands):
        stem, lower_cur, upper_cur, grad_low, grad_up = operands
        empty_grads = tuple((jnp.zeros(weight.shape, jnp.float32) for weight in weights))
        return (
            jnp.zeros_like(lower_cur),
            jnp.zeros_like(upper_cur),
            jnp.zeros_like(grad_low),
            jnp.zeros_like(grad_up),
            empty_grads,
            jnp.zeros(lower_cur.shape, jnp.float32),
        )

    def advance(turn_number, carry):
        received, totals, stem_acc = carry
        position = turn_number - (groups - 1 - column_index)
        active = jnp.logical_and(position >= 0, position < total_pieces)
        chosen = jnp.clip(position, 0, total_pieces - 1)
        lower_in = jnp.where(is_last, top_lower[chosen], received[0])
        upper_in = jnp.where(is_last, top_upper[chosen], received[1])
        grad_low_in = jnp.where(is_last, seed_lower[chosen].astype(jnp.float32), received[2])
        grad_up_in = jnp.where(is_last, seed_upper[chosen].astype(jnp.float32), received[3])
        outcome = lax.cond(
            active,
            column_work,
            skipped,
            (stem_input[chosen], lower_in, upper_in, grad_low_in, grad_up_in),
        )
        lower_prev, upper_prev, grad_low_prev, grad_up_prev, grads, d_stem = outcome
        totals = tuple((total + grad for total, grad in zip(totals, grads)))
        stem_acc = stem_acc.at[chosen].add(d_stem)
        received = shifted((lower_prev, upper_prev, grad_low_prev, grad_up_prev), "col", -1)
        return (received, totals, stem_acc)

    lower_zero = jnp.zeros((piece_lower, channels), jnp.float32)
    upper_zero = jnp.zeros((piece_upper, width_upper), jnp.float32)
    start_received = (lower_zero, upper_zero, lower_zero, upper_zero)
    start_totals = tuple((jnp.zeros(weight.shape, jnp.float32) for weight in weights))
    start_stem = jnp.zeros((total_pieces, piece_lower, channels), jnp.float32)
    received, totals, stem_acc = lax.fori_loop(
        0, total_pieces + groups - 1, advance, (start_received, start_totals, start_stem)
    )
    factor = 1.0 / math.sqrt(batches * rows_lower * lax.axis_size("dp"))
    scaled = tuple(((total * factor)[None] for total in totals))
    summed = (
        lax.psum_scatter(scaled[0], "dp", scatter_dimension=1, tiled=True),
        lax.psum_scatter(scaled[1], "dp", scatter_dimension=1, tiled=True),
        lax.psum_scatter(scaled[2], "dp", scatter_dimension=1, tiled=True),
        lax.psum_scatter(scaled[3], "dp", scatter_dimension=1, tiled=True),
        lax.psum_scatter(scaled[4], "dp", scatter_dimension=1, tiled=True),
        lax.psum_scatter(scaled[5], "dp", scatter_dimension=1, tiled=True),
    )
    stem_grad = lax.psum(stem_acc, "col")
    return (summed[0], summed[1], summed[2], summed[3], summed[4], summed[5], stem_grad)


def solution(mesh):
    in_specs = (
        P(None, "dp", None),
        P(None, "dp", None),
        P(None, "dp", None),
        P(None, "dp", None),
        P(None, "dp", None),
        P("col", None),
        P("col", None),
        P("col", None, None),
        P("col", None, None),
        P("col", None, None),
        P("col", None, None),
        P("col", None, None),
        P("col", None, None),
    )
    out_specs = (
        P("col", "dp", None),
        P("col", "dp", None),
        P("col", "dp", None),
        P("col", "dp", None),
        P("col", "dp", None),
        P("col", "dp", None),
        P(None, "dp", None),
    )
    return jax.shard_map(shards, mesh=mesh, in_specs=in_specs, out_specs=out_specs, check_vma=False)
```

profile of v0, /device:TPU:1, one launch (start us, length us, event | category | flops | bytes accessed | tf_op | source)
XLA Modules:
  0.0 1338.6 jit_solution(5890081681023642793)
XLA Ops:
  10.6 585.3 %while.37 = (s32[]{:T(128)}, f32[256,256]{1,0:T(8,128)S(1)}, f32[64,512]{1,0:T(8,128)}, f32[256,256]{1,0:T(8,128)}, f32[64,512]{1,0:T(8,128)S(1)}, /*index=5*/f3...) while((s32[]{:T(128)}, f32[256,256]{1,0:T(8,128)S(1)}, ...), condition=%wide.region_12.13_spmd.clone, body=%wide.region_0.12_spmd.clone.sunk | while | flops 1880310144 | bytes 217392624 | solution.py:206
  10.7 9.7 conditional.3
  26.3 5.5 select_add_fusion.16
  48.7 9.7 conditional.3
  64.4 6.8 select_add_fusion.16
  88.1 9.7 conditional.3
  103.7 6.8 select_add_fusion.16
  127.4 9.7 conditional.3
  143.0 6.8 select_add_fusion.16
  166.7 9.7 conditional.3
  182.4 6.8 select_add_fusion.16
  207.0 9.7 conditional.3
  222.6 6.8 select_add_fusion.16
  248.8 9.7 conditional.3
  264.5 6.8 select_add_fusion.16
  287.4 63.7 %collective-permute-done.1 = f32[64,512]{1,0:T(8,128)S(1)} collective-permute-done((f32[64,512]{1,0:T(8,128)S(1)}, f32[64,512]{1,0:T(8,128)S(1)}, u32[]{:S(2)}, u32[]{:S(2)}) %collective-permute-start.1) | collective-permute-done | bytes 131104 | tf_op jit(solution)/shard_map/while/body/eval_jaxpr/ppermute | solution.py:12
  354.6 28.9 %conditional.3 = (f32[256,256]{1,0:T(8,128)S(1)}, f32[64,512]{1,0:T(8,128)S(1)}, f32[256,256]{1,0:T(8,128)}, f32[64,512]{1,0:T(8,128)}, f32[512,256]{1,0:T(8,128...) conditional(s32[]{:T(128)} %convert_element_type.185, () %tuple.81, ...), branch_computations={%region_1.1_spmd, %region_2.10_spmd} | conditional | flops 1873625472 | bytes 100212096 | solution.py:189
  389.4 6.8 select_add_fusion.16
  415.6 28.9 %conditional.3 = (f32[256,256]{1,0:T(8,128)S(1)}, f32[64,512]{1,0:T(8,128)S(1)}, f32[256,256]{1,0:T(8,128)}, f32[64,512]{1,0:T(8,128)}, f32[512,256]{1,0:T(8,128...) conditional(s32[]{:T(128)} %convert_element_type.185, () %tuple.81, ...), branch_computations={%region_1.1_spmd, %region_2.10_spmd} | conditional | flops 1873625472 | bytes 100212096 | solution.py:189
  450.3 6.8 select_add_fusion.16
  476.6 28.9 %conditional.3 = (f32[256,256]{1,0:T(8,128)S(1)}, f32[64,512]{1,0:T(8,128)S(1)}, f32[256,256]{1,0:T(8,128)}, f32[64,512]{1,0:T(8,128)}, f32[512,256]{1,0:T(8,128...) conditional(s32[]{:T(128)} %convert_element_type.185, () %tuple.81, ...), branch_computations={%region_1.1_spmd, %region_2.10_spmd} | conditional | flops 1873625472 | bytes 100212096 | solution.py:189
  511.3 6.8 select_add_fusion.16
  537.5 28.9 %conditional.3 = (f32[256,256]{1,0:T(8,128)S(1)}, f32[64,512]{1,0:T(8,128)S(1)}, f32[256,256]{1,0:T(8,128)}, f32[64,512]{1,0:T(8,128)}, f32[512,256]{1,0:T(8,128...) conditional(s32[]{:T(128)} %convert_element_type.185, () %tuple.81, ...), branch_computations={%region_1.1_spmd, %region_2.10_spmd} | conditional | flops 1873625472 | bytes 100212096 | solution.py:189
  572.3 6.8 select_add_fusion.16
  603.7 4.9 multiply_bitcast_fusion.1
  608.7 4.6 multiply_bitcast_fusion
  613.4 110.4 %reduce-scatter.7.cloned.1.call-done = f32[1,16,256]{2,1,0:T(8,128)} async-done(((f32[1,512,256]{2,1,0:T(8,128)}), f32[1,16,256]{2,1,0:T(8,128)}) %reduce-scatter.7.cloned.1.call-update) | async-done | bytes 16400 | tf_op jit(solution)/shard_map/reduce_scatter | solution.py:212
  723.8 118.2 %reduce-scatter.11.cloned.1.call-done = f32[1,32,256]{2,1,0:T(8,128)} async-done(((f32[1,1024,256]{2,1,0:T(8,128)}), f32[1,32,256]{2,1,0:T(8,128)}) %reduce-scatter.11.cloned.1.call-update) | async-done | bytes 32784 | tf_op jit(solution)/shard_map/reduce_scatter | solution.py:214
  842.0 117.9 %reduce-scatter.9.cloned.1.call-done = f32[1,8,1024]{2,1,0:T(8,128)} async-done(((f32[1,256,1024]{2,1,0:T(8,128)}), f32[1,8,1024]{2,1,0:T(8,128)}) %reduce-scatter.9.cloned.1.call-update) | async-done | bytes 32784 | tf_op jit(solution)/shard_map/reduce_scatter | solution.py:213
  960.0 120.0 %reduce-scatter.13.cloned.1.call-done = f32[1,32,512]{2,1,0:T(8,128)} async-done(((f32[1,1024,512]{2,1,0:T(8,128)}), f32[1,32,512]{2,1,0:T(8,128)}) %reduce-scatter.13.cloned.1.call-update) | async-done | bytes 65552 | tf_op jit(solution)/shard_map/reduce_scatter | solution.py:215
  1080.0 124.2 %reduce-scatter.15.cloned.1.call-done = f32[1,16,2048]{2,1,0:T(8,128)} async-done(((f32[1,512,2048]{2,1,0:T(8,128)}), f32[1,16,2048]{2,1,0:T(8,128)}) %reduce-scatter.15.cloned.1.call-update) | async-done | bytes 131088 | tf_op jit(solution)/shard_map/reduce_scatter | solution.py:216
  1204.2 124.7 %reduce-scatter.17.cloned.1.call-done = f32[1,64,512]{2,1,0:T(8,128)} async-done(((f32[1,2048,512]{2,1,0:T(8,128)}), f32[1,64,512]{2,1,0:T(8,128)}) %reduce-scatter.17.cloned.1.call-update) | async-done | bytes 131088 | tf_op jit(solution)/shard_map/reduce_scatter | solution.py:217
  (952 shorter events, 456.9 us)
Async XLA Ops:
  8.0 715.8 %reduce-scatter.7.cloned.1.call-start = ((), (), s32[]{:S(2)}) async-start(), calls=%async_computation.6 | async-start | bytes 540672 | tf_op jit(solution)/shard_map/reduce_scatter | solution.py:212
  21.1 26.9 %collective-permute-start = (f32[256,256]{1,0:T(8,128)}, f32[256,256]{1,0:T(8,128)S(1)}, u32[]{:S(2)}, u32[]{:S(2)}) collective-permute-start(f32[256,256]{1,0:T(8,128)} %copy-done.32), channel_id=1, source_target_pairs={{32,0},{64,32},{96,64},{128,96},{160,128},{192,160},{224,192},{33,... | collective-permute-start | bytes 786440 | tf_op jit(solution)/shard_map/while/body/eval_jaxpr/ppermute | solution.py:12
  59.2 28.1 %collective-permute-start = (f32[256,256]{1,0:T(8,128)}, f32[256,256]{1,0:T(8,128)S(1)}, u32[]{:S(2)}, u32[]{:S(2)}) collective-permute-start(f32[256,256]{1,0:T(8,128)} %copy-done.32), channel_id=1, source_target_pairs={{32,0},{64,32},{96,64},{128,96},{160,128},{192,160},{224,192},{33,... | collective-permute-start | bytes 786440 | tf_op jit(solution)/shard_map/while/body/eval_jaxpr/ppermute | solution.py:12
  60.5 26.8 %collective-permute-start.2 = (f32[256,256]{1,0:T(8,128)}, f32[256,256]{1,0:T(8,128)S(1)}, u32[]{:S(2)}, u32[]{:S(2)}) collective-permute-start(f32[256,256]{1,0:T(8,128)} %get-tuple-element.1205), channel_id=1, source_target_pairs={{32,0},{64,32},{96,64},{128,96},{160,128},{192,160},{224,192},{33,... | collective-permute-start | bytes 786440 | tf_op jit(solution)/shard_map/while/body/eval_jaxpr/ppermute | solution.py:12
  98.5 28.1 %collective-permute-start = (f32[256,256]{1,0:T(8,128)}, f32[256,256]{1,0:T(8,128)S(1)}, u32[]{:S(2)}, u32[]{:S(2)}) collective-permute-start(f32[256,256]{1,0:T(8,128)} %copy-done.32), channel_id=1, source_target_pairs={{32,0},{64,32},{96,64},{128,96},{160,128},{192,160},{224,192},{33,... | collective-permute-start | bytes 786440 | tf_op jit(solution)/shard_map/while/body/eval_jaxpr/ppermute | solution.py:12
  99.8 26.8 %collective-permute-start.2 = (f32[256,256]{1,0:T(8,128)}, f32[256,256]{1,0:T(8,128)S(1)}, u32[]{:S(2)}, u32[]{:S(2)}) collective-permute-start(f32[256,256]{1,0:T(8,128)} %get-tuple-element.1205), channel_id=1, source_target_pairs={{32,0},{64,32},{96,64},{128,96},{160,128},{192,160},{224,192},{33,... | collective-permute-start | bytes 786440 | tf_op jit(solution)/shard_map/while/body/eval_jaxpr/ppermute | solution.py:12
  137.8 28.1 %collective-permute-start = (f32[256,256]{1,0:T(8,128)}, f32[256,256]{1,0:T(8,128)S(1)}, u32[]{:S(2)}, u32[]{:S(2)}) collective-permute-start(f32[256,256]{1,0:T(8,128)} %copy-done.32), channel_id=1, source_target_pairs={{32,0},{64,32},{96,64},{128,96},{160,128},{192,160},{224,192},{33,... | collective-permute-start | bytes 786440 | tf_op jit(solution)/shard_map/while/body/eval_jaxpr/ppermute | solution.py:12
  139.1 26.8 %collective-permute-start.2 = (f32[256,256]{1,0:T(8,128)}, f32[256,256]{1,0:T(8,128)S(1)}, u32[]{:S(2)}, u32[]{:S(2)}) collective-permute-start(f32[256,256]{1,0:T(8,128)} %get-tuple-element.1205), channel_id=1, source_target_pairs={{32,0},{64,32},{96,64},{128,96},{160,128},{192,160},{224,192},{33,... | collective-permute-start | bytes 786440 | tf_op jit(solution)/shard_map/while/body/eval_jaxpr/ppermute | solution.py:12
  177.2 29.1 %collective-permute-start = (f32[256,256]{1,0:T(8,128)}, f32[256,256]{1,0:T(8,128)S(1)}, u32[]{:S(2)}, u32[]{:S(2)}) collective-permute-start(f32[256,256]{1,0:T(8,128)} %copy-done.32), channel_id=1, source_target_pairs={{32,0},{64,32},{96,64},{128,96},{160,128},{192,160},{224,192},{33,... | collective-permute-start | bytes 786440 | tf_op jit(solution)/shard_map/while/body/eval_jaxpr/ppermute | solution.py:12
  178.4 27.8 %collective-permute-start.2 = (f32[256,256]{1,0:T(8,128)}, f32[256,256]{1,0:T(8,128)S(1)}, u32[]{:S(2)}, u32[]{:S(2)}) collective-permute-start(f32[256,256]{1,0:T(8,128)} %get-tuple-element.1205), channel_id=1, source_target_pairs={{32,0},{64,32},{96,64},{128,96},{160,128},{192,160},{224,192},{33,... | collective-permute-start | bytes 786440 | tf_op jit(solution)/shard_map/while/body/eval_jaxpr/ppermute | solution.py:12
  217.4 30.7 %collective-permute-start = (f32[256,256]{1,0:T(8,128)}, f32[256,256]{1,0:T(8,128)S(1)}, u32[]{:S(2)}, u32[]{:S(2)}) collective-permute-start(f32[256,256]{1,0:T(8,128)} %copy-done.32), channel_id=1, source_target_pairs={{32,0},{64,32},{96,64},{128,96},{160,128},{192,160},{224,192},{33,... | collective-permute-start | bytes 786440 | tf_op jit(solution)/shard_map/while/body/eval_jaxpr/ppermute | solution.py:12
  218.7 29.4 %collective-permute-start.2 = (f32[256,256]{1,0:T(8,128)}, f32[256,256]{1,0:T(8,128)S(1)}, u32[]{:S(2)}, u32[]{:S(2)}) collective-permute-start(f32[256,256]{1,0:T(8,128)} %get-tuple-element.1205), channel_id=1, source_target_pairs={{32,0},{64,32},{96,64},{128,96},{160,128},{192,160},{224,192},{33,... | collective-permute-start | bytes 786440 | tf_op jit(solution)/shard_map/while/body/eval_jaxpr/ppermute | solution.py:12
  221.3 26.8 %collective-permute-start.3 = (f32[64,512]{1,0:T(8,128)}, f32[64,512]{1,0:T(8,128)S(1)}, u32[]{:S(2)}, u32[]{:S(2)}) collective-permute-start(f32[64,512]{1,0:T(8,128)} %get-tuple-element.1206), channel_id=1, source_target_pairs={{32,0},{64,32},{96,64},{128,96},{160,128},{192,160},{224,192},{33,... | collective-permute-start | bytes 393224 | tf_op jit(solution)/shard_map/while/body/eval_jaxpr/ppermute | solution.py:12
  259.3 94.6 %collective-permute-start = (f32[256,256]{1,0:T(8,128)}, f32[256,256]{1,0:T(8,128)S(1)}, u32[]{:S(2)}, u32[]{:S(2)}) collective-permute-start(f32[256,256]{1,0:T(8,128)} %copy-done.32), channel_id=1, source_target_pairs={{32,0},{64,32},{96,64},{128,96},{160,128},{192,160},{224,192},{33,... | collective-permute-start | bytes 786440 | tf_op jit(solution)/shard_map/while/body/eval_jaxpr/ppermute | solution.py:12
  260.6 93.3 %collective-permute-start.2 = (f32[256,256]{1,0:T(8,128)}, f32[256,256]{1,0:T(8,128)S(1)}, u32[]{:S(2)}, u32[]{:S(2)}) collective-permute-start(f32[256,256]{1,0:T(8,128)} %get-tuple-element.1205), channel_id=1, source_target_pairs={{32,0},{64,32},{96,64},{128,96},{160,128},{192,160},{224,192},{33,... | collective-permute-start | bytes 786440 | tf_op jit(solution)/shard_map/while/body/eval_jaxpr/ppermute | solution.py:12
  261.9 89.2 %collective-permute-start.1 = (f32[64,512]{1,0:T(8,128)S(1)}, f32[64,512]{1,0:T(8,128)S(1)}, u32[]{:S(2)}, u32[]{:S(2)}) collective-permute-start(f32[64,512]{1,0:T(8,128)S(1)} %get-tuple-element.1204), channel_id=1, source_target_pairs={{32,0},{64,32},{96,64},{128,96},{160,128},{192,160},{224,192},{33,... | collective-permute-start | bytes 393224 | tf_op jit(solution)/shard_map/while/body/eval_jaxpr/ppermute | solution.py:12
  263.2 90.7 %collective-permute-start.3 = (f32[64,512]{1,0:T(8,128)}, f32[64,512]{1,0:T(8,128)S(1)}, u32[]{:S(2)}, u32[]{:S(2)}) collective-permute-start(f32[64,512]{1,0:T(8,128)} %get-tuple-element.1206), channel_id=1, source_target_pairs={{32,0},{64,32},{96,64},{128,96},{160,128},{192,160},{224,192},{33,... | collective-permute-start | bytes 393224 | tf_op jit(solution)/shard_map/while/body/eval_jaxpr/ppermute | solution.py:12
  384.2 30.7 %collective-permute-start = (f32[256,256]{1,0:T(8,128)}, f32[256,256]{1,0:T(8,128)S(1)}, u32[]{:S(2)}, u32[]{:S(2)}) collective-permute-start(f32[256,256]{1,0:T(8,128)} %copy-done.32), channel_id=1, source_target_pairs={{32,0},{64,32},{96,64},{128,96},{160,128},{192,160},{224,192},{33,... | collective-permute-start | bytes 786440 | tf_op jit(solution)/shard_map/while/body/eval_jaxpr/ppermute | solution.py:12
  385.5 29.4 %collective-permute-start.2 = (f32[256,256]{1,0:T(8,128)}, f32[256,256]{1,0:T(8,128)S(1)}, u32[]{:S(2)}, u32[]{:S(2)}) collective-permute-start(f32[256,256]{1,0:T(8,128)} %get-tuple-element.1205), channel_id=1, source_target_pairs={{32,0},{64,32},{96,64},{128,96},{160,128},{192,160},{224,192},{33,... | collective-permute-start | bytes 786440 | tf_op jit(solution)/shard_map/while/body/eval_jaxpr/ppermute | solution.py:12
  445.1 30.7 %collective-permute-start = (f32[256,256]{1,0:T(8,128)}, f32[256,256]{1,0:T(8,128)S(1)}, u32[]{:S(2)}, u32[]{:S(2)}) collective-permute-start(f32[256,256]{1,0:T(8,128)} %copy-done.32), channel_id=1, source_target_pairs={{32,0},{64,32},{96,64},{128,96},{160,128},{192,160},{224,192},{33,... | collective-permute-start | bytes 786440 | tf_op jit(solution)/shard_map/while/body/eval_jaxpr/ppermute | solution.py:12
  446.4 29.4 %collective-permute-start.2 = (f32[256,256]{1,0:T(8,128)}, f32[256,256]{1,0:T(8,128)S(1)}, u32[]{:S(2)}, u32[]{:S(2)}) collective-permute-start(f32[256,256]{1,0:T(8,128)} %get-tuple-element.1205), channel_id=1, source_target_pairs={{32,0},{64,32},{96,64},{128,96},{160,128},{192,160},{224,192},{33,... | collective-permute-start | bytes 786440 | tf_op jit(solution)/shard_map/while/body/eval_jaxpr/ppermute | solution.py:12
  449.0 26.8 %collective-permute-start.3 = (f32[64,512]{1,0:T(8,128)}, f32[64,512]{1,0:T(8,128)S(1)}, u32[]{:S(2)}, u32[]{:S(2)}) collective-permute-start(f32[64,512]{1,0:T(8,128)} %get-tuple-element.1206), channel_id=1, source_target_pairs={{32,0},{64,32},{96,64},{128,96},{160,128},{192,160},{224,192},{33,... | collective-permute-start | bytes 393224 | tf_op jit(solution)/shard_map/while/body/eval_jaxpr/ppermute | solution.py:12
  506.1 30.6 %collective-permute-start = (f32[256,256]{1,0:T(8,128)}, f32[256,256]{1,0:T(8,128)S(1)}, u32[]{:S(2)}, u32[]{:S(2)}) collective-permute-start(f32[256,256]{1,0:T(8,128)} %copy-done.32), channel_id=1, source_target_pairs={{32,0},{64,32},{96,64},{128,96},{160,128},{192,160},{224,192},{33,... | collective-permute-start | bytes 786440 | tf_op jit(solution)/shard_map/while/body/eval_jaxpr/ppermute | solution.py:12
  507.4 29.3 %collective-permute-start.2 = (f32[256,256]{1,0:T(8,128)}, f32[256,256]{1,0:T(8,128)S(1)}, u32[]{:S(2)}, u32[]{:S(2)}) collective-permute-start(f32[256,256]{1,0:T(8,128)} %get-tuple-element.1205), channel_id=1, source_target_pairs={{32,0},{64,32},{96,64},{128,96},{160,128},{192,160},{224,192},{33,... | collective-permute-start | bytes 786440 | tf_op jit(solution)/shard_map/while/body/eval_jaxpr/ppermute | solution.py:12
  567.1 28.1 %collective-permute-start = (f32[256,256]{1,0:T(8,128)}, f32[256,256]{1,0:T(8,128)S(1)}, u32[]{:S(2)}, u32[]{:S(2)}) collective-permute-start(f32[256,256]{1,0:T(8,128)} %copy-done.32), channel_id=1, source_target_pairs={{32,0},{64,32},{96,64},{128,96},{160,128},{192,160},{224,192},{33,... | collective-permute-start | bytes 786440 | tf_op jit(solution)/shard_map/while/body/eval_jaxpr/ppermute | solution.py:12
  568.3 26.8 %collective-permute-start.2 = (f32[256,256]{1,0:T(8,128)}, f32[256,256]{1,0:T(8,128)S(1)}, u32[]{:S(2)}, u32[]{:S(2)}) collective-permute-start(f32[256,256]{1,0:T(8,128)} %get-tuple-element.1205), channel_id=1, source_target_pairs={{32,0},{64,32},{96,64},{128,96},{160,128},{192,160},{224,192},{33,... | collective-permute-start | bytes 786440 | tf_op jit(solution)/shard_map/while/body/eval_jaxpr/ppermute | solution.py:12
  597.9 125.9 %all-reduce.2.cloned.1.call-start = ((), (), s32[]{:S(2)}) async-start(), calls=%async_computation.12 | async-start | bytes 2097152 | tf_op jit(solution)/shard_map/psum | solution.py:219
  598.5 243.5 %reduce-scatter.11.cloned.1.call-start = ((), (), s32[]{:S(2)}) async-start(), calls=%async_computation.8 | async-start | bytes 1081344 | tf_op jit(solution)/shard_map/reduce_scatter | solution.py:214
  600.9 359.1 %reduce-scatter.9.cloned.1.call-start = ((), (), s32[]{:S(2)}) async-start(), calls=%async_computation.7 | async-start | bytes 1081344 | tf_op jit(solution)/shard_map/reduce_scatter | solution.py:213
  602.1 477.9 %reduce-scatter.13.cloned.1.call-start = ((), (), s32[]{:S(2)}) async-start(), calls=%async_computation.9 | async-start | bytes 2162688 | tf_op jit(solution)/shard_map/reduce_scatter | solution.py:215
  603.7 600.5 %reduce-scatter.15.cloned.1.call-start = ((), (), s32[]{:S(2)}) async-start(), calls=%async_computation.10 | async-start | bytes 4325376 | tf_op jit(solution)/shard_map/reduce_scatter | solution.py:216
  608.7 720.2 %reduce-scatter.17.cloned.1.call-start = ((), (), s32[]{:S(2)}) async-start(), calls=%async_computation.11 | async-start | bytes 4325376 | tf_op jit(solution)/shard_map/reduce_scatter | solution.py:217
  (279 other events, 1530.9 us)
Sparse Core Ops, SparseCore 0:
  598.1 125.7 reduce-scatter.6
  727.0 114.9 reduce-scatter.10
  845.1 114.8 reduce-scatter.8
  963.1 116.8 reduce-scatter.12
  1082.9 121.1 reduce-scatter.14
  1207.1 121.6 reduce-scatter.16
Sparse Core Ops, SparseCore 1:
  601.1 98.8 all-reduce.1
where the time goes:
time: 1350 us; the launch traced here: 1340 us
  waiting for transfers between devices  794 us (59%)
  other arithmetic  246 us (18%)
  local copies, waits for them, and re-layouts  131 us (10%)
  matrix products  91.3 us (7%)
  starting transfers between devices  57 us (4%)
  between operations  15.6 us (1%)
    add x66, other arithmetic, advance(): totals = tuple((total + grad for total, grad in zip(totals, grads)))  180 us
    reduce_scatter x1, waiting for transfers between devices, shards(): lax.psum_scatter(scaled[5], 'dp', scatter_dimension=1, tiled=True)  125 us
    reduce_scatter x1, waiting for transfers between devices, shards(): lax.psum_scatter(scaled[4], 'dp', scatter_dimension=1, tiled=True)  124 us
    reduce_scatter x1, waiting for transfers between devices, shards(): lax.psum_scatter(scaled[3], 'dp', scatter_dimension=1, tiled=True)  120 us
    reduce_scatter x1, waiting for transfers between devices, shards(): lax.psum_scatter(scaled[2], 'dp', scatter_dimension=1, tiled=True)  118 us
    reduce_scatter x1, waiting for transfers between devices, shards(): lax.psum_scatter(scaled[1], 'dp', scatter_dimension=1, tiled=True)  118 us
    reduce_scatter x1, waiting for transfers between devices, shards(): lax.psum_scatter(scaled[0], 'dp', scatter_dimension=1, tiled=True)  110 us
    ppermute x44, waiting for transfers between devices, shifted(): return lax.ppermute(array, axis, pairs)  77.7 us
  transfers between devices with their start and end apart: 51, of which 13 were waited for; matrix products, arithmetic and copies ran while one was open for 17% of the time, Pallas kernels for 0%

commit v1 on v0

v1 whole, which is shorter than its diff:
```python
import functools
import math

import jax
import jax.numpy as jnp
from jax import lax
from jax.experimental import pallas as pl
from jax.experimental.pallas import tpu as pltpu
from jax.sharding import PartitionSpec as P

MESH = pl.DeviceIdType.MESH
F32 = jnp.float32
BF16 = jnp.bfloat16
EPS = 1e-06
PIECES = 8
FOLD = 4
VMEM_LIMIT = 60 << 20


def product(left, right):
    return jnp.dot(left, right, preferred_element_type=F32)


def right_outer(left, right):
    return lax.dot_general(left, right, (((1,), (1,)), ((), ())), preferred_element_type=F32)


def left_outer(left, right):
    return lax.dot_general(left, right, (((0,), (0,)), ((), ())), preferred_element_type=F32)


def inverse_rms(square_sum, width):
    return lax.rsqrt(square_sum * (1.0 / width) + EPS)


def row_sum(values):
    return jnp.sum(values, axis=-1, keepdims=True)


def norm_back(values, inverse, cotangent):
    normed = values * inverse
    mean = row_sum(cotangent * normed) * (1.0 / values.shape[-1])
    return inverse * (cotangent - normed * mean)


def gate(hidden):
    return 0.5 * jnp.tanh(0.5 * hidden) + 0.5


def column_kernel(
    pieces, columns,
    stem, top_lower, top_upper, seed_lower, seed_upper, gain_lower, gain_upper,
    lift, inner, outer, merge, expand, reduce,
    folded_out, merged_out, ugate_out, gu_out, duh_out, dmerged_out,
    ucast_out, dlift_out, normed_out, lgate_out, gl_out, dlh_out, stem_out,
    in_low, in_up, in_glow, in_gup, out_low, out_up, out_glow, out_gup,
    slope_up, slope_low, stem_half, top_half, seed_half, part_half, send_sem, recv_sem, load_sem,
):
    column = lax.axis_index("col")
    first = column == columns - 1
    has_next = column > 0
    ru = in_up.shape[1]
    rl = FOLD * ru
    channels = in_low.shape[-1]
    lanes = channels // 2

    def half_copies(array, halves, index):
        return [
            pltpu.make_async_copy(
                array.at[:, pl.ds(h * lanes, lanes)], halves.at[h], load_sem.at[index, h]
            )
            for h in range(2)
        ]

    loads = half_copies(top_lower, top_half, 0)
    loads += half_copies(stem, stem_half, 1)
    loads += half_copies(seed_lower, seed_half, 2)
    for load in loads:
        load.start()

    def strided(halves, start):
        return jnp.concatenate(
            [halves[h, pl.ds(start, ru, stride=FOLD), :] for h in range(2)], axis=1
        )

    barrier = pltpu.get_barrier_semaphore()

    @pl.when(jnp.logical_not(first))
    def _():
        pl.semaphore_signal(barrier, inc=1, device_id={"col": column + 1}, device_id_type=MESH)

    @pl.when(has_next)
    def _():
        pl.semaphore_wait(barrier, 1)

    streams = ((out_low, in_low), (out_up, in_up), (out_glow, in_glow), (out_gup, in_gup))

    def copy(kind, p):
        source, target = streams[kind]
        return pltpu.make_async_remote_copy(
            src_ref=source.at[p],
            dst_ref=target.at[p],
            send_sem=send_sem.at[kind, p],
            recv_sem=recv_sem.at[kind, p],
            device_id={"col": column - 1},
            device_id_type=MESH,
        )

    def push(kind, p):
        @pl.when(has_next)
        def _():
            copy(kind, p).start()

    def arrive(kind, p):
        @pl.when(jnp.logical_not(first))
        def _():
            copy(kind, p).wait_recv()

    inverse_gain_up = 1.0 / gain_upper[...]
    inverse_gain_low = 1.0 / gain_lower[...]

    for load in loads:
        load.wait()

    def piece(p, carry):
        base = p * rl

        @pl.when(first)
        def _():
            for i in range(FOLD):
                in_low[p, i] = strided(top_half, base + i)
                in_glow[p, i] = strided(seed_half, base + i)
            in_up[p] = top_upper[p]
            in_gup[p] = seed_upper[p].astype(F32)

        arrive(0, p)
        low = [in_low[p, i] for i in range(FOLD)]
        squares = sum(row_sum(v * v) for v in low)
        inverse_fold = inverse_rms(squares, FOLD * channels)
        folded = jnp.concatenate([(v * inverse_fold).astype(BF16) for v in low], axis=1)
        folded_out[p] = folded
        merged = product(folded, merge[...])
        inverse_merged = inverse_rms(row_sum(merged * merged), merged.shape[-1])
        merged_cast = (merged * inverse_merged).astype(BF16)
        merged_out[p] = merged_cast
        branch = jnp.zeros_like(merged)
        wide = expand.shape[1]
        step = min(512, wide)
        for c in range(0, wide, step):
            hidden = product(merged_cast, expand[:, c:c + step])
            g = gate(hidden)
            gated = (hidden * g).astype(BF16)
            ugate_out[p, :, c:c + step] = gated
            slope_up[:, c:c + step] = g * (1.0 + hidden * (1.0 - g))
            branch = branch + product(gated, reduce[c:c + step, :])
        arrive(1, p)
        upper_prev = (in_up[p] - (merged + branch)) * inverse_gain_up
        out_up[p] = upper_prev
        push(1, p)
        upper_cast = upper_prev.astype(BF16)
        ucast_out[p] = upper_cast
        lifted = product(upper_cast, lift[...])
        mixed = jnp.concatenate(
            [strided(stem_half, base + i) + lifted for i in range(FOLD)], axis=0
        )
        inverse_mixed = inverse_rms(row_sum(mixed * mixed), channels)
        normed = (mixed * inverse_mixed).astype(BF16)
        normed_out[p] = normed
        wide_low = inner.shape[1]
        lower_branch = jnp.zeros((rl, channels), F32)
        step_low = min(256, wide_low)
        for c in range(0, wide_low, step_low):
            hidden = product(normed, inner[:, c:c + step_low])
            g = gate(hidden)
            gated = (hidden * g).astype(BF16)
            lgate_out[p, :, c:c + step_low] = gated
            slope_low[:, c:c + step_low] = g * (1.0 + hidden * (1.0 - g))
            lower_branch = lower_branch + product(gated, outer[c:c + step_low, :])
        for i in range(FOLD):
            out_low[p, i] = (in_low[p, i] - lower_branch[i * ru:(i + 1) * ru]) * inverse_gain_low
        push(0, p)

        arrive(3, p)
        grad_up = in_gup[p]
        gu = grad_up.astype(BF16)
        gu_out[p] = gu
        d_cast = jnp.zeros_like(merged)
        for c in range(0, wide, step):
            d_gate = right_outer(gu, reduce[c:c + step, :])
            duh = (slope_up[:, c:c + step] * d_gate).astype(BF16)
            duh_out[p, :, c:c + step] = duh
            d_cast = d_cast + right_outer(duh, expand[:, c:c + step])
        dmerged = (grad_up + norm_back(merged, inverse_merged, d_cast)).astype(BF16)
        dmerged_out[p] = dmerged
        d_fold = right_outer(dmerged, merge[...])
        low = [in_low[p, i] * inverse_fold for i in range(FOLD)]
        parts = [d_fold[:, i * channels:(i + 1) * channels] for i in range(FOLD)]
        mean = sum(row_sum(a * b) for a, b in zip(low, parts)) * (1.0 / (FOLD * channels))
        arrive(2, p)
        total = []
        for i in range(FOLD):
            t = in_glow[p, i] + inverse_fold * (parts[i] - low[i] * mean)
            out_glow[p, i] = gain_lower[...] * t
            total.append(t.astype(BF16))
        push(2, p)
        gl = jnp.concatenate(total, axis=0)
        gl_out[p] = gl
        d_normed = jnp.zeros((rl, channels), F32)
        for c in range(0, wide_low, step_low):
            d_gate = right_outer(gl, outer[c:c + step_low, :])
            dlh = (slope_low[:, c:c + step_low] * d_gate).astype(BF16)
            dlh_out[p, :, c:c + step_low] = dlh
            d_normed = d_normed + right_outer(dlh, inner[:, c:c + step_low])
        d_mixed = norm_back(mixed, inverse_mixed, d_normed)
        d_lift = jnp.zeros((ru, channels), F32)
        for i in range(FOLD):
            part = d_mixed[i * ru:(i + 1) * ru]
            for h in range(2):
                part_half[h, pl.ds(base + i, ru, stride=FOLD), :] = part[:, h * lanes:(h + 1) * lanes]
            d_lift = d_lift + part
        d_lift = d_lift.astype(BF16)
        dlift_out[p] = d_lift
        out_gup[p] = gain_upper[...] * grad_up + right_outer(d_lift, lift[...])
        push(3, p)
        return carry

    lax.fori_loop(0, pieces, piece, 0)

    stores = [
        pltpu.make_async_copy(
            part_half.at[h], stem_out.at[:, pl.ds(h * lanes, lanes)], load_sem.at[3, h]
        )
        for h in range(2)
    ]
    for store in stores:
        store.start()

    @pl.when(has_next)
    def _():
        def drain(p, carry):
            for kind in range(4):
                copy(kind, p).wait_send()
            return carry

        lax.fori_loop(0, pieces, drain, 0)

    for store in stores:
        store.wait()


def run_columns(stem, top_lower, top_upper, seed_lower, seed_upper, gain_lower, gain_upper, weights):
    pieces = PIECES
    lower_rows, channels = stem.shape
    upper_rows, width = top_upper.shape
    ru = upper_rows // pieces
    rl = lower_rows // pieces
    hidden_up = weights[4].shape[1]
    hidden_low = weights[1].shape[1]
    fold_width = FOLD * channels
    shape = lambda rows, cols, kind=BF16: jax.ShapeDtypeStruct((pieces, rows, cols), kind)
    outs = (
        shape(ru, fold_width), shape(ru, width), shape(ru, hidden_up), shape(ru, width),
        shape(ru, hidden_up), shape(ru, width), shape(ru, width), shape(ru, channels),
        shape(rl, channels), shape(rl, hidden_low), shape(rl, channels), shape(rl, hidden_low),
        jax.ShapeDtypeStruct((lower_rows, channels), F32),
    )
    low_slot = pltpu.VMEM((pieces, FOLD, ru, channels), F32)
    up_slot = pltpu.VMEM((pieces, ru, width), F32)
    vmem = pl.BlockSpec(memory_space=pltpu.VMEM)
    away = pl.BlockSpec(memory_space=pl.ANY)
    half = pltpu.VMEM((2, lower_rows, channels // 2), F32)
    results = pl.pallas_call(
        functools.partial(column_kernel, pieces, lax.axis_size("col")),
        out_shape=outs,
        in_specs=[away, away, vmem, away] + [vmem] * 9,
        out_specs=tuple([vmem] * 12 + [away]),
        scratch_shapes=[
            low_slot, up_slot, low_slot, up_slot, low_slot, up_slot, low_slot, up_slot,
            pltpu.VMEM((ru, hidden_up), F32), pltpu.VMEM((rl, hidden_low), F32),
            half, half, half, half,
            pltpu.SemaphoreType.DMA((4, pieces)), pltpu.SemaphoreType.DMA((4, pieces)),
            pltpu.SemaphoreType.DMA((4, 2)),
        ],
        compiler_params=pltpu.CompilerParams(
            collective_id=0, has_side_effects=True, vmem_limit_bytes=VMEM_LIMIT
        ),
        name="columns",
    )(
        stem.astype(F32), top_lower, top_upper.reshape(pieces, ru, width),
        seed_lower.astype(F32), seed_upper.reshape(pieces, ru, width),
        gain_lower, gain_upper, *weights,
    )
    flat = [r.reshape(-1, r.shape[-1]) for r in results]
    return flat


SLAB = 256


def scatter_kernel(
    columns, depth, factor, plan, rows_a,
    folded, merged, ugate, gu, duh, dmerged, ucast, dlift, normed, lgate, gl, dlh, stem_part,
    lift_out, inner_out, outer_out, merge_out, expand_out, reduce_out, stem_out,
    part, near, side, last, ring, stem_got,
    near_sem, side_sem, last_sem, ring_sem, stem_sem, stem_full_sem,
):
    column = lax.axis_index("col")
    place = lax.axis_index("dp")
    z, y, core = place // 4, (place // 2) % 2, place % 2
    at = lambda z, y, core: {"dp": z * 4 + y * 2 + core}
    peer = at(z, y, 1 - core)
    across = at(z, 1 - y, core)
    toward = (at((z + 1) % depth, y, core), at((z + depth - 1) % depth, y, core))
    others = [(column + d) % columns for d in range(1, columns)]

    barrier = pltpu.get_barrier_semaphore()
    for target in (peer, across) + toward + tuple({"col": o} for o in others):
        pl.semaphore_signal(barrier, inc=1, device_id=target, device_id_type=MESH)
    pl.semaphore_wait(barrier, 3 + columns)

    def remote(source, target, send, recv, device):
        return pltpu.make_async_remote_copy(
            src_ref=source, dst_ref=target, send_sem=send, recv_sem=recv,
            device_id=device, device_id_type=MESH,
        )

    def weight_grad(name):
        left, right, start = {
            "reduce": (ugate, gu, plan["reduce"]), "expand": (merged, duh, plan["expand"]),
            "merge": (folded, dmerged, plan["merge"]), "outer": (lgate, gl, plan["outer"]),
            "inner": (normed, dlh, plan["inner"]), "lift": (ucast, dlift, plan["lift"]),
        }[name]
        height, width = left.shape[1], right.shape[1]
        block = height // (4 * depth)
        for top in range(0, height, SLAB):
            grad = left_outer(left[:, top:top + SLAB], right[...])
            count = SLAB // (4 * block)
            z0 = top // (4 * block)
            for slab in range(width // SLAB):
                piece = grad[:, slab * SLAB:(slab + 1) * SLAB].reshape(count, 2, 2, block, SLAB)
                rows = slice(start + slab * block, start + (slab + 1) * block)
                for yb in range(2):
                    part[yb * depth + z0:yb * depth + z0 + count, :, rows, :] = piece[:, yb]

    def near_copy(group):
        start, rows, _ = group
        return remote(
            part.at[:, 1 - core, pl.ds(start, rows)], near.at[:, pl.ds(start, rows)],
            near_sem.at[0, start // 16], near_sem.at[1, start // 16], peer,
        )

    def side_copy(group):
        start, rows, _ = group
        return remote(
            near.at[pl.ds((1 - y) * depth, depth), pl.ds(start, rows)],
            side.at[:, pl.ds(start - rows_a, rows)],
            side_sem.at[0, start // 16], side_sem.at[1, start // 16], across,
        )

    def flows(group):
        start, rows, first = group
        if first:
            return [(way, start, rows, way, start) for way in range(2)]
        half = rows // 2
        slot = rows_a + (start - rows_a) // 2
        return [(way, start + way * half, half, y, slot) for way in range(2)]

    def block_at(way, step):
        if way == 0:
            return (z + 2 * depth - 1 - step) % depth
        return (z + 1 + step) % depth

    def gathered(group, flow, step, zb):
        way, start, rows, yb, slot = flow
        value = near[yb * depth + zb, start:start + rows] + part[yb * depth + zb, core, start:start + rows]
        if not group[2]:
            value = value + side[zb, start - rows_a:start - rows_a + rows]
        return value

    def ring_copy(flow, step):
        way, start, rows, yb, slot = flow
        return remote(
            near.at[yb * depth + block_at(way, step), pl.ds(start, rows)],
            ring.at[way, step, pl.ds(slot, rows)],
            ring_sem.at[0, way, step, slot // 16], ring_sem.at[1, way, step, slot // 16], toward[way],
        )

    def ring_step(group, step, opening):
        for flow in flows(group):
            way, start, rows, yb, slot = flow
            zb = block_at(way, step)
            value = gathered(group, flow, step, zb)
            if not opening:
                ring_copy(flow, step - 1).wait_recv()
                value = value + ring[way, step - 1, slot:slot + rows]
            near[yb * depth + zb, start:start + rows] = value
            ring_copy(flow, step).start()

    def ring_end(group):
        for flow in flows(group):
            way, start, rows, yb, slot = flow
            ring_copy(flow, depth - 2).wait_recv()
            value = gathered(group, flow, depth - 1, z)
            near[yb * depth + z, start:start + rows] = value + ring[way, depth - 2, slot:slot + rows]

    def side_open(group):
        start, rows, _ = group

        def add(zb, carry):
            b = (1 - y) * depth + zb
            near[b, start:start + rows] = near[b, start:start + rows] + part[b, core, start:start + rows]
            return carry

        lax.fori_loop(0, depth, add, 0)
        side_copy(group).start()

    a1, a2 = (0, plan["outer"], True), (plan["outer"], rows_a - plan["outer"], True)
    b1 = (rows_a, plan["merge"] - rows_a, False)
    b2 = (plan["merge"], part.shape[2] - plan["merge"], False)

    weight_grad("reduce")
    near_copy(a1).start()
    weight_grad("expand")
    near_copy(b1).start()
    near_copy(a1).wait_recv()
    ring_step(a1, 0, True)
    weight_grad("merge")
    near_copy(b2).start()
    near_copy(b1).wait_recv()
    side_open(b1)
    for name in ("outer", "inner", "lift"):
        weight_grad(name)
    near_copy(a2).start()
    near_copy(b2).wait_recv()
    side_open(b2)
    near_copy(a2).wait_recv()
    ring_step(a2, 0, True)

    seg = stem_part.shape[0] // columns

    def stem_copy(owner, slot_of):
        return remote(
            stem_part.at[pl.ds(owner * seg, seg)], stem_got.at[0, slot_of],
            stem_sem.at[0, owner], stem_sem.at[1, slot_of], {"col": owner},
        )

    def stem_spread(target, slot_of):
        return remote(
            stem_got.at[1, column], stem_got.at[1, slot_of],
            stem_full_sem.at[0, target], stem_full_sem.at[1, slot_of], {"col": target},
        )

    for other in others:
        stem_copy(other, column).start()

    def first_rings(step, carry):
        ring_step(a1, step, False)
        ring_step(a2, step, False)
        return carry

    lax.fori_loop(1, depth - 1, first_rings, 0)

    for group in (b1, b2):
        side_copy(group).wait_recv()
        ring_step(group, 0, True)
    ring_end(a1)
    ring_end(a2)
    last_copy = remote(
        near.at[(1 - y) * depth + z, pl.ds(0, rows_a)], last, last_sem.at[0], last_sem.at[1], across
    )
    last_copy.start()

    total = stem_part[pl.ds(pl.multiple_of(column * seg, seg), seg), :]
    for other in others:
        stem_copy(other, other).wait_recv()
        total = total + stem_got[0, other]
    stem_got[1, column] = total
    for other in others:
        stem_spread(other, column).start()

    def second_rings(step, carry):
        ring_step(b1, step, False)
        ring_step(b2, step, False)
        return carry

    lax.fori_loop(1, depth - 1, second_rings, 0)

    def emit(out, name, value):
        block, width = out.shape
        start = plan[name] - value[1]
        for slab in range(width // SLAB):
            out[:, slab * SLAB:(slab + 1) * SLAB] = (
                value[0][start + slab * block:start + (slab + 1) * block] * factor
            )

    last_copy.wait_recv()
    mine = near[y * depth + z, 0:rows_a] + last[...]
    for out, name in ((reduce_out, "reduce"), (outer_out, "outer"), (inner_out, "inner"), (lift_out, "lift")):
        emit(out, name, (mine, 0))
    ring_end(b1)
    ring_end(b2)
    mine = near[y * depth + z, rows_a:part.shape[2]]
    for out, name in ((expand_out, "expand"), (merge_out, "merge")):
        emit(out, name, (mine, rows_a))

    stem_out[pl.ds(pl.multiple_of(column * seg, seg), seg), :] = stem_got[1, column]
    for other in others:
        stem_spread(other, other).wait_recv()
        stem_out[pl.ds(pl.multiple_of(other * seg, seg), seg), :] = stem_got[1, other]

    for group in (a1, a2, b1, b2):
        near_copy(group).wait_send()
    for group in (b1, b2):
        side_copy(group).wait_send()
    last_copy.wait_send()

    def drain(step, carry):
        for group in (a1, a2, b1, b2):
            for flow in flows(group):
                ring_copy(flow, step).wait_send()
        return carry

    lax.fori_loop(0, depth - 1, drain, 0)
    for other in others:
        stem_copy(other, column).wait_send()
        stem_spread(other, column).wait_send()


def run_scatter(saved, shapes, factor):
    devices = lax.axis_size("dp")
    columns = lax.axis_size("col")
    depth = devices // 4
    blocks = [(rows // devices, cols) for rows, cols in shapes]
    heights = {
        name: block * (cols // SLAB)
        for name, (block, cols) in zip(("lift", "inner", "outer", "merge", "expand", "reduce"), blocks)
    }
    plan, height = {}, 0
    for name in ("reduce", "outer", "inner", "lift", "expand", "merge"):
        plan[name] = height
        height += heights[name]
    rows_a = plan["expand"]
    slots = rows_a + (height - rows_a) // 2
    stem_part = saved[-1]
    outs = [jax.ShapeDtypeStruct(b, F32) for b in blocks]
    outs.append(jax.ShapeDtypeStruct(stem_part.shape, F32))
    seg = stem_part.shape[0] // columns
    vmem = pl.BlockSpec(memory_space=pltpu.VMEM)
    dma = pltpu.SemaphoreType.DMA
    return pl.pallas_call(
        functools.partial(scatter_kernel, columns, depth, factor, plan, rows_a),
        out_shape=tuple(outs),
        in_specs=[vmem] * 13,
        out_specs=tuple(vmem for _ in outs),
        scratch_shapes=[
            pltpu.VMEM((2 * depth, 2, height, SLAB), F32),
            pltpu.VMEM((2 * depth, height, SLAB), F32),
            pltpu.VMEM((depth, height - rows_a, SLAB), F32),
            pltpu.VMEM((rows_a, SLAB), F32),
            pltpu.VMEM((2, depth - 1, slots, SLAB), F32),
            pltpu.VMEM((2, columns, seg, stem_part.shape[1]), F32),
            dma((2, 32)), dma((2, 32)), dma((2,)), dma((2, 2, depth, 32)),
            dma((2, columns)), dma((2, columns)),
        ],
        compiler_params=pltpu.CompilerParams(
            collective_id=1, has_side_effects=True, vmem_limit_bytes=VMEM_LIMIT
        ),
        name="scatter",
    )(*saved)


def shards(stem_input, top_lower, top_upper, seed_lower, seed_upper, gamma_lower, gamma_upper, *weights):
    flat = lambda array: array.reshape(-1, array.shape[-1])
    weights = [w[0] for w in weights]
    saved = run_columns(
        flat(stem_input), flat(top_lower), flat(top_upper), flat(seed_lower), flat(seed_upper),
        gamma_lower, gamma_upper, weights,
    )
    factor = 1.0 / math.sqrt(saved[-1].shape[0] * lax.axis_size("dp"))
    results = run_scatter(saved, [w.shape for w in weights], factor)
    return tuple(r[None] for r in results[:6]) + (results[6].reshape(stem_input.shape),)


def solution(mesh):
    spread = P(None, "dp", None)
    gains = P("col", None)
    table = P("col", None, None)
    in_specs = (spread,) * 5 + (gains,) * 2 + (table,) * 6
    out_specs = (P("col", "dp", None),) * 6 + (spread,)
    return jax.shard_map(shards, mesh=mesh, in_specs=in_specs, out_specs=out_specs, check_vma=False)
```

time: 1350 us -> 250 us (0.19)
  waiting for transfers between devices: 794 us -> 0 us
  other arithmetic: 246 us -> 2.7 us
  Pallas kernels: 0 us -> 233 us
  local copies, waits for them, and re-layouts: 131 us -> 11 us
  matrix products: 91.3 us -> 0 us
  starting transfers between devices: 57 us -> 0 us
  between operations: 15.6 us -> 0.65 us
    reduce_scatter x6 -> x0, waiting for transfers between devices: 715 us -> none  [the longest x1 125 us: shards(): lax.psum_scatter(scaled[5], 'dp', scatter_dimension=1, tiled=True)]
    pallas_call x0 -> x2, Pallas kernels: none -> 233 us  [the longest x1 135 us: run_columns(): pl.pallas_call(functools.partial(column_kernel, pieces, lax.axis_size('co...]
    add x66 -> x0, other arithmetic: 180 us -> none  [advance(): totals = tuple((total + grad for total, grad in zip(totals, grads)))]
    dot_general x72 -> x0, matrix products: 91.3 us -> none  [the longest x24 40 us: left_outer(): lax.dot_general(left_side, right_side, (((0,), (0,)), ((), ())), preferre...]
    ppermute x44 -> x0, waiting for transfers between devices: 77.7 us -> none  [shifted(): return lax.ppermute(array, axis, pairs)]
    another operation x81 -> x0, local copies, waits for them, and re-layouts: 69.3 us -> none
    ppermute x44 -> x0, starting transfers between devices: 56.7 us -> none  [shifted(): return lax.ppermute(array, axis, pairs)]
    while x308 -> x0, local copies, waits for them, and re-layouts: 51 us -> none
  transfers between devices with their start and end apart: 51 -> 0, of which waited for: 13 -> 0; matrix products, arithmetic and copies ran while one was open for 17% -> 0% of each run, Pallas kernels for 0% -> 0%
where the time goes in v1:
time: 250 us; the launch traced here: 247 us
  Pallas kernels  233 us (93%)
  local copies, waits for them, and re-layouts  11 us (4%)
  other arithmetic  2.7 us (1%)
    pallas_call x1, Pallas kernels, run_columns(): pl.pallas_call(functools.partial(column_kernel, pieces, lax.axis_size('co...  135 us
    pallas_call x1, Pallas kernels, run_scatter(): pl.pallas_call(functools.partial(scatter_kernel, columns, depth, factor,...  97.3 us
    unnamed x7, local copies, waits for them, and re-layouts  11 us

profile of v1, /device:TPU:1, one launch (start us, length us, event | category | flops | bytes accessed | tf_op | source)
XLA Modules:
  0.0 247.0 jit_solution(6253195280263651879)
XLA Ops:
  0.6 2.7 %bitcast_convert_fusion = (f32[1024,256]{1,0:T(8,128)}, f32[1024,256]{1,0:T(8,128)}) fusion(bf16[4,256,256]{2,1,0:T(8,128)(2,1)} %param.16, bf16[4,256,256]{2,1,0:T(8,128)(2,1)} %param.13), kind=kLoop, calls=%fused_computation | loop fusion | flops 524288 | bytes 3145728 | tf_op jit(solution)/shard_map/convert_element_type | solution.py:290
  3.3 135.3 %columns.1 = (bf16[8,32,1024]{2,1,0:T(8,128)(2,1)}, bf16[8,32,512]{2,1,0:T(8,128)(2,1)}, bf16[8,32,2048]{2,1,0:T(8,128)(2,1)}, bf16[8,32,512]{2,1,0:T(8,128)(2,1...) custom-call(f32[1024,256]{1,0:T(8,128)} %get-tuple-element.48.stem, ...), custom_call_target="tpu_custom_call" | custom-call | tf_op jit(solution)/shard_map/columns/pallas_call | solution.py:272
  138.6 97.3 %scatter.1 = (f32[16,256]{1,0:T(8,128)}, f32[8,1024]{1,0:T(8,128)}, f32[32,256]{1,0:T(8,128)}, f32[32,512]{1,0:T(8,128)}, f32[16,2048]{1,0:T(8,128)}, /*index=5*/f32[64,512]{1,0:T(8,128)}, f32[1024,256]{1,0:T(8,128)}) custom-call(bf16[256,1024]{1,0:T(8,128)(2,1)} %bitcast.46, bf16[256,512]{1,0:T(8,128)(2,1)} %bitcast.51, bf16[256,2048]{1,0:T(8,128)(2,1)} %bitcast.40, ...), custom_call_target="tpu_custom_call" | custom-call | tf_op jit(solution)/shard_map/scatter/pallas_call | solution.py:550
  236.0 1.3 copy.27
  237.3 1.4 copy.28
  238.7 1.4 copy.29
  240.1 1.5 copy.30
  241.5 1.6 copy.31
  243.1 1.6 copy.32
  244.7 2.3 copy.33

commit v2 on v1

--- a/solution.py
+++ b/solution.py
@@ -12,7 +12,7 @@
 F32 = jnp.float32
 BF16 = jnp.bfloat16
 EPS = 1e-06
-PIECES = 8
+PIECES = 16
 FOLD = 4
 VMEM_LIMIT = 60 << 20
 
@@ -54,7 +54,7 @@
     folded_out, merged_out, ugate_out, gu_out, duh_out, dmerged_out,
     ucast_out, dlift_out, normed_out, lgate_out, gl_out, dlh_out, stem_out,
     in_low, in_up, in_glow, in_gup, out_low, out_up, out_glow, out_gup,
-    slope_up, slope_low, stem_half, top_half, seed_half, part_half, send_sem, recv_sem, load_sem,
+    slope_up, slope_low, top_half, part_half, send_sem, recv_sem, load_sem,
 ):
     column = lax.axis_index("col")
     first = column == columns - 1
@@ -73,10 +73,11 @@
         ]
 
     loads = half_copies(top_lower, top_half, 0)
-    loads += half_copies(stem, stem_half, 1)
-    loads += half_copies(seed_lower, seed_half, 2)
-    for load in loads:
-        load.start()
+
+    @pl.when(first)
+    def _():
+        for load in loads:
+            load.start()
 
     def strided(halves, start):
         return jnp.concatenate(
@@ -106,10 +107,11 @@
             device_id_type=MESH,
         )
 
-    def push(kind, p):
+    def push(kinds, p):
         @pl.when(has_next)
         def _():
-            copy(kind, p).start()
+            for kind in kinds:
+                copy(kind, p).start()
 
     def arrive(kind, p):
         @pl.when(jnp.logical_not(first))
@@ -119,17 +121,24 @@
     inverse_gain_up = 1.0 / gain_upper[...]
     inverse_gain_low = 1.0 / gain_lower[...]
 
-    for load in loads:
-        load.wait()
+    @pl.when(first)
+    def _():
+        for load in loads:
+            load.wait()
+
+    spot = lax.broadcasted_iota(jnp.int32, (rl, rl), 0)
+    token = lax.broadcasted_iota(jnp.int32, (rl, rl), 1)
+    order = jnp.where(token == (spot % ru) * FOLD + spot // ru, 1.0, 0.0).astype(BF16)
 
     def piece(p, carry):
         base = p * rl
 
         @pl.when(first)
         def _():
+            seeds = product(order, seed_lower[p])
             for i in range(FOLD):
                 in_low[p, i] = strided(top_half, base + i)
-                in_glow[p, i] = strided(seed_half, base + i)
+                in_glow[p, i] = seeds[i * ru:(i + 1) * ru]
             in_up[p] = top_upper[p]
             in_gup[p] = seed_upper[p].astype(F32)
 
@@ -145,7 +154,7 @@
         merged_out[p] = merged_cast
         branch = jnp.zeros_like(merged)
         wide = expand.shape[1]
-        step = min(512, wide)
+        step = wide
         for c in range(0, wide, step):
             hidden = product(merged_cast, expand[:, c:c + step])
             g = gate(hidden)
@@ -156,19 +165,16 @@
         arrive(1, p)
         upper_prev = (in_up[p] - (merged + branch)) * inverse_gain_up
         out_up[p] = upper_prev
-        push(1, p)
         upper_cast = upper_prev.astype(BF16)
         ucast_out[p] = upper_cast
         lifted = product(upper_cast, lift[...])
-        mixed = jnp.concatenate(
-            [strided(stem_half, base + i) + lifted for i in range(FOLD)], axis=0
-        )
+        mixed = product(order, stem[p]) + jnp.concatenate([lifted] * FOLD, axis=0)
         inverse_mixed = inverse_rms(row_sum(mixed * mixed), channels)
         normed = (mixed * inverse_mixed).astype(BF16)
         normed_out[p] = normed
         wide_low = inner.shape[1]
         lower_branch = jnp.zeros((rl, channels), F32)
-        step_low = min(256, wide_low)
+        step_low = wide_low
         for c in range(0, wide_low, step_low):
             hidden = product(normed, inner[:, c:c + step_low])
             g = gate(hidden)
@@ -178,7 +184,7 @@
             lower_branch = lower_branch + product(gated, outer[c:c + step_low, :])
         for i in range(FOLD):
             out_low[p, i] = (in_low[p, i] - lower_branch[i * ru:(i + 1) * ru]) * inverse_gain_low
-        push(0, p)
+        push((0, 1), p)
 
         arrive(3, p)
         grad_up = in_gup[p]
@@ -202,7 +208,6 @@
             t = in_glow[p, i] + inverse_fold * (parts[i] - low[i] * mean)
             out_glow[p, i] = gain_lower[...] * t
             total.append(t.astype(BF16))
-        push(2, p)
         gl = jnp.concatenate(total, axis=0)
         gl_out[p] = gl
         d_normed = jnp.zeros((rl, channels), F32)
@@ -221,14 +226,14 @@
         d_lift = d_lift.astype(BF16)
         dlift_out[p] = d_lift
         out_gup[p] = gain_upper[...] * grad_up + right_outer(d_lift, lift[...])
-        push(3, p)
+        push((3, 2), p)
         return carry
 
     lax.fori_loop(0, pieces, piece, 0)
 
     stores = [
         pltpu.make_async_copy(
-            part_half.at[h], stem_out.at[:, pl.ds(h * lanes, lanes)], load_sem.at[3, h]
+            part_half.at[h], stem_out.at[:, pl.ds(h * lanes, lanes)], load_sem.at[1, h]
         )
         for h in range(2)
     ]
@@ -272,22 +277,22 @@
     results = pl.pallas_call(
         functools.partial(column_kernel, pieces, lax.axis_size("col")),
         out_shape=outs,
-        in_specs=[away, away, vmem, away] + [vmem] * 9,
+        in_specs=[vmem, away] + [vmem] * 11,
         out_specs=tuple([vmem] * 12 + [away]),
         scratch_shapes=[
             low_slot, up_slot, low_slot, up_slot, low_slot, up_slot, low_slot, up_slot,
             pltpu.VMEM((ru, hidden_up), F32), pltpu.VMEM((rl, hidden_low), F32),
-            half, half, half, half,
+            half, half,
             pltpu.SemaphoreType.DMA((4, pieces)), pltpu.SemaphoreType.DMA((4, pieces)),
-            pltpu.SemaphoreType.DMA((4, 2)),
+            pltpu.SemaphoreType.DMA((2, 2)),
         ],
         compiler_params=pltpu.CompilerParams(
             collective_id=0, has_side_effects=True, vmem_limit_bytes=VMEM_LIMIT
         ),
         name="columns",
     )(
-        stem.astype(F32), top_lower, top_upper.reshape(pieces, ru, width),
-        seed_lower.astype(F32), seed_upper.reshape(pieces, ru, width),
+        stem.reshape(pieces, rl, channels), top_lower, top_upper.reshape(pieces, ru, width),
+        seed_lower.reshape(pieces, rl, channels), seed_upper.reshape(pieces, ru, width),
         gain_lower, gain_upper, *weights,
     )
     flat = [r.reshape(-1, r.shape[-1]) for r in results]
@@ -300,9 +305,9 @@
 def scatter_kernel(
     columns, depth, factor, plan, rows_a,
     folded, merged, ugate, gu, duh, dmerged, ucast, dlift, normed, lgate, gl, dlh, stem_part,
-    lift_out, inner_out, outer_out, merge_out, expand_out, reduce_out, stem_out,
-    part, near, side, last, ring, stem_got,
-    near_sem, side_sem, last_sem, ring_sem, stem_sem, stem_full_sem,
+    packed_out, stem_out,
+    part, near, side, last, ring, stem_got, stem_half, stem_full,
+    near_sem, side_sem, last_sem, ring_sem, row_sem, half_sem, full_sem, out_sem,
 ):
     column = lax.axis_index("col")
     place = lax.axis_index("dp")
@@ -311,12 +316,16 @@
     peer = at(z, y, 1 - core)
     across = at(z, 1 - y, core)
     toward = (at((z + 1) % depth, y, core), at((z + depth - 1) % depth, y, core))
-    others = [(column + d) % columns for d in range(1, columns)]
+    row = columns // 2
+    x, high = column % row, column // row
+    mates = [(x + d) % row for d in range(1, row)]
+    mate = lambda other: {"col": high * row + other}
+    mirror = {"col": (1 - high) * row + x}
 
     barrier = pltpu.get_barrier_semaphore()
-    for target in (peer, across) + toward + tuple({"col": o} for o in others):
+    for target in (peer, across, mirror) + toward + tuple(mate(o) for o in mates):
         pl.semaphore_signal(barrier, inc=1, device_id=target, device_id_type=MESH)
-    pl.semaphore_wait(barrier, 3 + columns)
+    pl.semaphore_wait(barrier, 4 + row)
 
     def remote(source, target, send, recv, device):
         return pltpu.make_async_remote_copy(
@@ -342,6 +351,10 @@
                 for yb in range(2):
                     part[yb * depth + z0:yb * depth + z0 + count, :, rows, :] = piece[:, yb]
 
+    a1, a2 = (0, plan["outer"], True), (plan["outer"], rows_a - plan["outer"], True)
+    b1 = (rows_a, plan["merge"] - rows_a, False)
+    b2 = (plan["merge"], part.shape[2] - plan["merge"], False)
+
     def near_copy(group):
         start, rows, _ = group
         return remote(
@@ -359,49 +372,63 @@
 
     def flows(group):
         start, rows, first = group
-        if first:
-            return [(way, start, rows, way, start) for way in range(2)]
-        half = rows // 2
-        slot = rows_a + (start - rows_a) // 2
-        return [(way, start + way * half, half, y, slot) for way in range(2)]
-
-    def block_at(way, step):
+        found = []
+        for lane in range(2):
+            for way in range(2):
+                steps = depth // 2 if way == lane else depth // 2 - 1
+                if first:
+                    found.append((way, lane, steps, start, rows, lane, start))
+                else:
+                    half = rows // 2
+                    slot = rows_a + (start - rows_a) // 2
+                    found.append((way, lane, steps, start + lane * half, half, y, slot))
+        return found
+
+    def block_at(flow, step):
+        way, steps = flow[0], flow[2]
         if way == 0:
-            return (z + 2 * depth - 1 - step) % depth
-        return (z + 1 + step) % depth
-
-    def gathered(group, flow, step, zb):
-        way, start, rows, yb, slot = flow
+            return (z + steps - step) % depth
+        return (z + depth - steps + step) % depth
+
+    def gathered(group, flow, zb):
+        way, lane, steps, start, rows, yb, slot = flow
         value = near[yb * depth + zb, start:start + rows] + part[yb * depth + zb, core, start:start + rows]
         if not group[2]:
             value = value + side[zb, start - rows_a:start - rows_a + rows]
         return value
 
     def ring_copy(flow, step):
-        way, start, rows, yb, slot = flow
+        way, lane, steps, start, rows, yb, slot = flow
         return remote(
-            near.at[yb * depth + block_at(way, step), pl.ds(start, rows)],
-            ring.at[way, step, pl.ds(slot, rows)],
-            ring_sem.at[0, way, step, slot // 16], ring_sem.at[1, way, step, slot // 16], toward[way],
-        )
-
-    def ring_step(group, step, opening):
+            near.at[yb * depth + block_at(flow, step), pl.ds(start, rows)],
+            ring.at[way, lane, step, pl.ds(slot, rows)],
+            ring_sem.at[0, way, lane, step, slot // 16], ring_sem.at[1, way, lane, step, slot // 16],
+            toward[way],
+        )
+
+    def ring_step(group, step):
         for flow in flows(group):
-            way, start, rows, yb, slot = flow
-            zb = block_at(way, step)
-            value = gathered(group, flow, step, zb)
-            if not opening:
+            way, lane, steps, start, rows, yb, slot = flow
+            if step >= steps:
+                continue
+            zb = block_at(flow, step)
+            value = gathered(group, flow, zb)
+            if step > 0:
                 ring_copy(flow, step - 1).wait_recv()
-                value = value + ring[way, step - 1, slot:slot + rows]
+                value = value + ring[way, lane, step - 1, slot:slot + rows]
             near[yb * depth + zb, start:start + rows] = value
             ring_copy(flow, step).start()
 
     def ring_end(group):
-        for flow in flows(group):
-            way, start, rows, yb, slot = flow
-            ring_copy(flow, depth - 2).wait_recv()
-            value = gathered(group, flow, depth - 1, z)
-            near[yb * depth + z, start:start + rows] = value + ring[way, depth - 2, slot:slot + rows]
+        found = flows(group)
+        for lane in range(2):
+            pair = [flow for flow in found if flow[1] == lane]
+            way, lane, steps, start, rows, yb, slot = pair[0]
+            value = gathered(group, pair[0], z)
+            for flow in pair:
+                ring_copy(flow, flow[2] - 1).wait_recv()
+                value = value + ring[flow[0], lane, flow[2] - 1, slot:slot + rows]
+            near[yb * depth + z, start:start + rows] = value
 
     def side_open(group):
         start, rows, _ = group
@@ -418,112 +445,114 @@
     b1 = (rows_a, plan["merge"] - rows_a, False)
     b2 = (plan["merge"], part.shape[2] - plan["merge"], False)
 
+    quarter = stem_part.shape[0] // row
+    half = quarter // 2
+    span = lambda index, size: pl.ds(pl.multiple_of(index * size, size), size)
+
+    def row_copy(target, slot):
+        return remote(
+            stem_part.at[span(target, quarter)], stem_got.at[slot],
+            row_sem.at[0, target], row_sem.at[1, slot], mate(target),
+        )
+
+    half_copy = remote(
+        stem_half.at[0, span(1 - high, half)], stem_half.at[1, pl.ds(0, half)],
+        half_sem.at[0], half_sem.at[1], mirror,
+    )
+
+    def back_copy(part_of):
+        ref = stem_full.at[x, span(part_of, half)]
+        return remote(ref, ref, half_sem.at[2], half_sem.at[3], mirror)
+
+    def full_copy(target, slot):
+        ref = stem_full.at[slot]
+        return remote(ref, ref, full_sem.at[0, target], full_sem.at[1, slot], mate(target))
+
+    def stem_rows():
+        total = stem_part[span(x, quarter), :]
+        for other in mates:
+            row_copy(other, other).wait_recv()
+            total = total + stem_got[other]
+        stem_half[0] = total
+        half_copy.start()
+
+    def stem_mirror():
+        half_copy.wait_recv()
+        stem_full[x, span(high, half), :] = stem_half[0, span(high, half), :] + stem_half[1, 0:half]
+        back_copy(high).start()
+
+    def stem_spread():
+        back_copy(1 - high).wait_recv()
+        for other in mates:
+            full_copy(other, x).start()
+
+    for other in mates:
+        row_copy(other, x).start()
+    weight_grad("expand")
+    near_copy(b1).start()
     weight_grad("reduce")
     near_copy(a1).start()
-    weight_grad("expand")
-    near_copy(b1).start()
-    near_copy(a1).wait_recv()
-    ring_step(a1, 0, True)
+    near_copy(b1).wait_recv()
+    side_open(b1)
     weight_grad("merge")
     near_copy(b2).start()
-    near_copy(b1).wait_recv()
-    side_open(b1)
+    near_copy(a1).wait_recv()
+    ring_step(a1, 0)
     for name in ("outer", "inner", "lift"):
         weight_grad(name)
     near_copy(a2).start()
     near_copy(b2).wait_recv()
     side_open(b2)
     near_copy(a2).wait_recv()
-    ring_step(a2, 0, True)
-
-    seg = stem_part.shape[0] // columns
-
-    def stem_copy(owner, slot_of):
-        return remote(
-            stem_part.at[pl.ds(owner * seg, seg)], stem_got.at[0, slot_of],
-            stem_sem.at[0, owner], stem_sem.at[1, slot_of], {"col": owner},
-        )
-
-    def stem_spread(target, slot_of):
-        return remote(
-            stem_got.at[1, column], stem_got.at[1, slot_of],
-            stem_full_sem.at[0, target], stem_full_sem.at[1, slot_of], {"col": target},
-        )
-
-    for other in others:
-        stem_copy(other, column).start()
-
-    def first_rings(step, carry):
-        ring_step(a1, step, False)
-        ring_step(a2, step, False)
-        return carry
-
-    lax.fori_loop(1, depth - 1, first_rings, 0)
-
-    for group in (b1, b2):
-        side_copy(group).wait_recv()
-        ring_step(group, 0, True)
+    ring_step(a2, 0)
+    ring_step(a1, 1)
+    ring_step(a2, 1)
+    ring_step(a1, 2)
+    ring_step(a2, 2)
+    stem_rows()
+    side_copy(b1).wait_recv()
+    ring_step(b1, 0)
+    ring_step(a1, 3)
+    ring_step(a2, 3)
+    stem_mirror()
+    ring_step(b1, 1)
     ring_end(a1)
     ring_end(a2)
     last_copy = remote(
         near.at[(1 - y) * depth + z, pl.ds(0, rows_a)], last, last_sem.at[0], last_sem.at[1], across
     )
     last_copy.start()
-
-    total = stem_part[pl.ds(pl.multiple_of(column * seg, seg), seg), :]
-    for other in others:
-        stem_copy(other, other).wait_recv()
-        total = total + stem_got[0, other]
-    stem_got[1, column] = total
-    for other in others:
-        stem_spread(other, column).start()
-
-    def second_rings(step, carry):
-        ring_step(b1, step, False)
-        ring_step(b2, step, False)
-        return carry
-
-    lax.fori_loop(1, depth - 1, second_rings, 0)
-
-    def emit(out, name, value):
-        block, width = out.shape
-        start = plan[name] - value[1]
-        for slab in range(width // SLAB):
-            out[:, slab * SLAB:(slab + 1) * SLAB] = (
-                value[0][start + slab * block:start + (slab + 1) * block] * factor
-            )
-
+    stem_spread()
+    side_copy(b2).wait_recv()
+    ring_step(b2, 0)
+    for step in range(2, depth // 2):
+        ring_step(b1, step)
+        ring_step(b2, step - 1)
+    ring_step(b2, depth // 2 - 1)
+    for other in mates:
+        full_copy(other, other).wait_recv()
+    stem_store = pltpu.make_async_copy(stem_full, stem_out, out_sem)
+    stem_store.start()
     last_copy.wait_recv()
-    mine = near[y * depth + z, 0:rows_a] + last[...]
-    for out, name in ((reduce_out, "reduce"), (outer_out, "outer"), (inner_out, "inner"), (lift_out, "lift")):
-        emit(out, name, (mine, 0))
+    packed_out[0:rows_a] = (near[y * depth + z, 0:rows_a] + last[...]) * factor
     ring_end(b1)
     ring_end(b2)
-    mine = near[y * depth + z, rows_a:part.shape[2]]
-    for out, name in ((expand_out, "expand"), (merge_out, "merge")):
-        emit(out, name, (mine, rows_a))
-
-    stem_out[pl.ds(pl.multiple_of(column * seg, seg), seg), :] = stem_got[1, column]
-    for other in others:
-        stem_spread(other, other).wait_recv()
-        stem_out[pl.ds(pl.multiple_of(other * seg, seg), seg), :] = stem_got[1, other]
+    packed_out[rows_a:] = near[y * depth + z, rows_a:] * factor
 
     for group in (a1, a2, b1, b2):
         near_copy(group).wait_send()
+        for flow in flows(group):
+            for step in range(flow[2]):
+                ring_copy(flow, step).wait_send()
     for group in (b1, b2):
         side_copy(group).wait_send()
     last_copy.wait_send()
-
-    def drain(step, carry):
-        for group in (a1, a2, b1, b2):
-            for flow in flows(group):
-                ring_copy(flow, step).wait_send()
-        return carry
-
-    lax.fori_loop(0, depth - 1, drain, 0)
-    for other in others:
-        stem_copy(other, column).wait_send()
-        stem_spread(other, column).wait_send()
+    half_copy.wait_send()
+    back_copy(high).wait_send()
+    for other in mates:
+        row_copy(other, x).wait_send()
+        full_copy(other, x).wait_send()
+    stem_store.wait()
 
 
 def run_scatter(saved, shapes, factor):
@@ -541,32 +570,53 @@
         height += heights[name]
     rows_a = plan["expand"]
     slots = rows_a + (height - rows_a) // 2
+    row = columns // 2
     stem_part = saved[-1]
-    outs = [jax.ShapeDtypeStruct(b, F32) for b in blocks]
-    outs.append(jax.ShapeDtypeStruct(stem_part.shape, F32))
-    seg = stem_part.shape[0] // columns
+    quarter = (stem_part.shape[0] // row, stem_part.shape[1])
+    full = (row,) + quarter
     vmem = pl.BlockSpec(memory_space=pltpu.VMEM)
+    away = pl.BlockSpec(memory_space=pl.ANY)
     dma = pltpu.SemaphoreType.DMA
-    return pl.pallas_call(
+    packed, stem = pl.pallas_call(
         functools.partial(scatter_kernel, columns, depth, factor, plan, rows_a),
-        out_shape=tuple(outs),
+        out_shape=(jax.ShapeDtypeStruct((height, SLAB), F32), jax.ShapeDtypeStruct(full, F32)),
         in_specs=[vmem] * 13,
-        out_specs=tuple(vmem for _ in outs),
+        out_specs=(vmem, away),
         scratch_shapes=[
             pltpu.VMEM((2 * depth, 2, height, SLAB), F32),
             pltpu.VMEM((2 * depth, height, SLAB), F32),
             pltpu.VMEM((depth, height - rows_a, SLAB), F32),
             pltpu.VMEM((rows_a, SLAB), F32),
-            pltpu.VMEM((2, depth - 1, slots, SLAB), F32),
-            pltpu.VMEM((2, columns, seg, stem_part.shape[1]), F32),
-            dma((2, 32)), dma((2, 32)), dma((2,)), dma((2, 2, depth, 32)),
-            dma((2, columns)), dma((2, columns)),
+            pltpu.VMEM((2, 2, depth // 2, slots, SLAB), F32),
+            pltpu.VMEM(full, F32), pltpu.VMEM((2,) + quarter, F32), pltpu.VMEM(full, F32),
+            dma((2, 32)), dma((2, 32)), dma((2,)), dma((2, 2, 2, depth // 2, 32)),
+            dma((2, row)), dma((4,)), dma((2, row)), dma,
         ],
         compiler_params=pltpu.CompilerParams(
             collective_id=1, has_side_effects=True, vmem_limit_bytes=VMEM_LIMIT
         ),
         name="scatter",
     )(*saved)
+    names = ("lift", "inner", "outer", "merge", "expand", "reduce")
+
+    def finish(packed_ref, stem_ref, *rest):
+        outs, stem_to = rest[:6], rest[6]
+        stem_to[...] = stem_ref[...]
+        for name, out in zip(names, outs):
+            block, width = out.shape
+            for slab in range(width // SLAB):
+                start = plan[name] + slab * block
+                out[:, slab * SLAB:(slab + 1) * SLAB] = packed_ref[start:start + block]
+
+    outs = [jax.ShapeDtypeStruct(b, F32) for b in blocks] + [jax.ShapeDtypeStruct(full, F32)]
+    return pl.pallas_call(
+        finish,
+        out_shape=tuple(outs),
+        in_specs=[vmem, vmem],
+        out_specs=tuple([vmem] * 7),
+        compiler_params=pltpu.CompilerParams(vmem_limit_bytes=VMEM_LIMIT),
+        name="finish",
+    )(packed, stem)
 
 
 def shards(stem_input, top_lower, top_upper, seed_lower, seed_upper, gamma_lower, gamma_upper, *weights):

time: 250 us -> 212 us (0.85)
  Pallas kernels: 233 us -> 211 us
  local copies, waits for them, and re-layouts: 11 us -> 0 us
  other arithmetic: 2.7 us -> 0 us
    pallas_call x1, Pallas kernels: 135 us -> 122 us  [run_columns(): pl.pallas_call(functools.partial(column_kernel, pieces, lax.axis_size('co...]
    unnamed x7 -> x0, local copies, waits for them, and re-layouts: 11 us -> none
    pallas_call x1, Pallas kernels: 97.3 us -> 86.4 us  [run_scatter(): pl.pallas_call(functools.partial(scatter_kernel, columns, depth, factor,...]
    convert_element_type x1 -> x0, other arithmetic: 2.7 us -> none  [run_columns(): seed_lower.astype(F32)]
where the time goes in v2:
time: 212 us; the launch traced here: 211 us
  Pallas kernels  211 us (100%)
    pallas_call x1, Pallas kernels, run_columns(): pl.pallas_call(functools.partial(column_kernel, pieces, lax.axis_size('co...  122 us
    pallas_call x1, Pallas kernels, run_scatter(): pl.pallas_call(functools.partial(scatter_kernel, columns, depth, factor,...  86.4 us

profile of v2, /device:TPU:1, one launch (start us, length us, event | category | flops | bytes accessed | tf_op | source)
XLA Modules:
  0.0 211.4 jit_solution(5609530337778004067)
XLA Ops:
  0.6 121.8 %columns.1 = (bf16[16,16,1024]{2,1,0:T(8,128)(2,1)}, bf16[16,16,512]{2,1,0:T(8,128)(2,1)}, bf16[16,16,2048]{2,1,0:T(8,128)(2,1)}, bf16[16,16,512]{2,1,0:T(8,128)...) custom-call(bf16[16,64,256]{2,1,0:T(8,128)(2,1)} %bitcast.37, ...), custom_call_target="tpu_custom_call" | custom-call | tf_op jit(solution)/shard_map/columns/pallas_call | solution.py:277
  122.5 86.4 %scatter.1 = (f32[400,256]{1,0:T(8,128)}, f32[4,256,256]{2,1,0:T(8,128)}) custom-call(bf16[256,1024]{1,0:T(8,128)(2,1)} %bitcast.42, bf16[256,512]{1,0:T(8,128)(2,1)} %bitcast.47, bf16[256,2048]{1,0:T(8,128)(2,1)} %bitcast.33, bf16[256,512]{1,0:T(8,128)(2,1)} %bitcast.48, bf16[256,2048]{1,0:T(8,128)(2,1)} %bitcast.34, bf16[256,512]{1,0:T(8,128)(2,1)} %bitcast.49, ...), custom_call_target="tpu_custom_call" | custom-call | tf_op jit(solution)/shard_map/scatter/pallas_call | solution.py:580
  208.9 2.5 %finish.1 = (f32[16,256]{1,0:T(8,128)}, f32[8,1024]{1,0:T(8,128)}, f32[32,256]{1,0:T(8,128)}, f32[32,512]{1,0:T(8,128)}, f32[16,2048]{1,0:T(8,128)}, /*index=5*/f32[64,512]{1,0:T(8,128)}, f32[4,256,256]{2,1,0:T(8,128)}) custom-call(f32[400,256]{1,0:T(8,128)} %get-tuple-element.42.packed_ref, f32[4,256,256]{2,1,0:T(8,128)} %get-tuple-element.43.stem_ref), custom_call_target="tpu_custom_call" | custom-call | tf_op jit(solution)/shard_map/finish/pallas_call | solution.py:612

commit v3 on v2

--- a/solution.py
+++ b/solution.py
@@ -52,9 +52,9 @@
     stem, top_lower, top_upper, seed_lower, seed_upper, gain_lower, gain_upper,
     lift, inner, outer, merge, expand, reduce,
     folded_out, merged_out, ugate_out, gu_out, duh_out, dmerged_out,
-    ucast_out, dlift_out, normed_out, lgate_out, gl_out, dlh_out, stem_out,
+    ucast_out, dlift_out, normed_out, lgate_out, gl_out, dlh_out, part_half,
     in_low, in_up, in_glow, in_gup, out_low, out_up, out_glow, out_gup,
-    slope_up, slope_low, top_half, part_half, send_sem, recv_sem, load_sem,
+    slope_up, slope_low, top_half, send_sem, recv_sem, load_sem,
 ):
     column = lax.axis_index("col")
     first = column == columns - 1
@@ -64,15 +64,15 @@
     channels = in_low.shape[-1]
     lanes = channels // 2
 
-    def half_copies(array, halves, index):
+    def half_copies(array, halves):
         return [
             pltpu.make_async_copy(
-                array.at[:, pl.ds(h * lanes, lanes)], halves.at[h], load_sem.at[index, h]
+                array.at[:, pl.ds(h * lanes, lanes)], halves.at[h], load_sem.at[h]
             )
             for h in range(2)
         ]
 
-    loads = half_copies(top_lower, top_half, 0)
+    loads = half_copies(top_lower, top_half)
 
     @pl.when(first)
     def _():
@@ -83,16 +83,6 @@
         return jnp.concatenate(
             [halves[h, pl.ds(start, ru, stride=FOLD), :] for h in range(2)], axis=1
         )
-
-    barrier = pltpu.get_barrier_semaphore()
-
-    @pl.when(jnp.logical_not(first))
-    def _():
-        pl.semaphore_signal(barrier, inc=1, device_id={"col": column + 1}, device_id_type=MESH)
-
-    @pl.when(has_next)
-    def _():
-        pl.semaphore_wait(barrier, 1)
 
     streams = ((out_low, in_low), (out_up, in_up), (out_glow, in_glow), (out_gup, in_gup))
 
@@ -107,15 +97,13 @@
             device_id_type=MESH,
         )
 
-    def push(kinds, p):
-        @pl.when(has_next)
-        def _():
+    def push(kinds, p, role):
+        if role != "last":
             for kind in kinds:
                 copy(kind, p).start()
 
-    def arrive(kind, p):
-        @pl.when(jnp.logical_not(first))
-        def _():
+    def arrive(kind, p, role):
+        if role != "first":
             copy(kind, p).wait_recv()
 
     inverse_gain_up = 1.0 / gain_upper[...]
@@ -130,11 +118,10 @@
     token = lax.broadcasted_iota(jnp.int32, (rl, rl), 1)
     order = jnp.where(token == (spot % ru) * FOLD + spot // ru, 1.0, 0.0).astype(BF16)
 
-    def piece(p, carry):
+    def piece(role, p, carry):
         base = p * rl
 
-        @pl.when(first)
-        def _():
+        if role == "first":
             seeds = product(order, seed_lower[p])
             for i in range(FOLD):
                 in_low[p, i] = strided(top_half, base + i)
@@ -142,7 +129,7 @@
             in_up[p] = top_upper[p]
             in_gup[p] = seed_upper[p].astype(F32)
 
-        arrive(0, p)
+        arrive(0, p, role)
         low = [in_low[p, i] for i in range(FOLD)]
         squares = sum(row_sum(v * v) for v in low)
         inverse_fold = inverse_rms(squares, FOLD * channels)
@@ -162,7 +149,7 @@
             ugate_out[p, :, c:c + step] = gated
             slope_up[:, c:c + step] = g * (1.0 + hidden * (1.0 - g))
             branch = branch + product(gated, reduce[c:c + step, :])
-        arrive(1, p)
+        arrive(1, p, role)
         upper_prev = (in_up[p] - (merged + branch)) * inverse_gain_up
         out_up[p] = upper_prev
         upper_cast = upper_prev.astype(BF16)
@@ -184,9 +171,9 @@
             lower_branch = lower_branch + product(gated, outer[c:c + step_low, :])
         for i in range(FOLD):
             out_low[p, i] = (in_low[p, i] - lower_branch[i * ru:(i + 1) * ru]) * inverse_gain_low
-        push((0, 1), p)
-
-        arrive(3, p)
+        push((0, 1), p, role)
+
+        arrive(3, p, role)
         grad_up = in_gup[p]
         gu = grad_up.astype(BF16)
         gu_out[p] = gu
@@ -202,7 +189,7 @@
         low = [in_low[p, i] * inverse_fold for i in range(FOLD)]
         parts = [d_fold[:, i * channels:(i + 1) * channels] for i in range(FOLD)]
         mean = sum(row_sum(a * b) for a, b in zip(low, parts)) * (1.0 / (FOLD * channels))
-        arrive(2, p)
+        arrive(2, p, role)
         total = []
         for i in range(FOLD):
             t = in_glow[p, i] + inverse_fold * (parts[i] - low[i] * mean)
@@ -226,19 +213,15 @@
         d_lift = d_lift.astype(BF16)
         dlift_out[p] = d_lift
         out_gup[p] = gain_upper[...] * grad_up + right_outer(d_lift, lift[...])
-        push((3, 2), p)
+        push((3, 2), p, role)
         return carry
 
-    lax.fori_loop(0, pieces, piece, 0)
-
-    stores = [
-        pltpu.make_async_copy(
-            part_half.at[h], stem_out.at[:, pl.ds(h * lanes, lanes)], load_sem.at[1, h]
-        )
-        for h in range(2)
-    ]
-    for store in stores:
-        store.start()
+    middle = jnp.logical_and(has_next, jnp.logical_not(first))
+    roles = (("first", first), ("middle", middle), ("last", jnp.logical_not(has_next)))
+    for role, here in roles:
+        @pl.when(here)
+        def _():
+            lax.fori_loop(0, pieces, functools.partial(piece, role), 0)
 
     @pl.when(has_next)
     def _():
@@ -248,55 +231,6 @@
             return carry
 
         lax.fori_loop(0, pieces, drain, 0)
-
-    for store in stores:
-        store.wait()
-
-
-def run_columns(stem, top_lower, top_upper, seed_lower, seed_upper, gain_lower, gain_upper, weights):
-    pieces = PIECES
-    lower_rows, channels = stem.shape
-    upper_rows, width = top_upper.shape
-    ru = upper_rows // pieces
-    rl = lower_rows // pieces
-    hidden_up = weights[4].shape[1]
-    hidden_low = weights[1].shape[1]
-    fold_width = FOLD * channels
-    shape = lambda rows, cols, kind=BF16: jax.ShapeDtypeStruct((pieces, rows, cols), kind)
-    outs = (
-        shape(ru, fold_width), shape(ru, width), shape(ru, hidden_up), shape(ru, width),
-        shape(ru, hidden_up), shape(ru, width), shape(ru, width), shape(ru, channels),
-        shape(rl, channels), shape(rl, hidden_low), shape(rl, channels), shape(rl, hidden_low),
-        jax.ShapeDtypeStruct((lower_rows, channels), F32),
-    )
-    low_slot = pltpu.VMEM((pieces, FOLD, ru, channels), F32)
-    up_slot = pltpu.VMEM((pieces, ru, width), F32)
-    vmem = pl.BlockSpec(memory_space=pltpu.VMEM)
-    away = pl.BlockSpec(memory_space=pl.ANY)
-    half = pltpu.VMEM((2, lower_rows, channels // 2), F32)
-    results = pl.pallas_call(
-        functools.partial(column_kernel, pieces, lax.axis_size("col")),
-        out_shape=outs,
-        in_specs=[vmem, away] + [vmem] * 11,
-        out_specs=tuple([vmem] * 12 + [away]),
-        scratch_shapes=[
-            low_slot, up_slot, low_slot, up_slot, low_slot, up_slot, low_slot, up_slot,
-            pltpu.VMEM((ru, hidden_up), F32), pltpu.VMEM((rl, hidden_low), F32),
-            half, half,
-            pltpu.SemaphoreType.DMA((4, pieces)), pltpu.SemaphoreType.DMA((4, pieces)),
-            pltpu.SemaphoreType.DMA((2, 2)),
-        ],
-        compiler_params=pltpu.CompilerParams(
-            collective_id=0, has_side_effects=True, vmem_limit_bytes=VMEM_LIMIT
-        ),
-        name="columns",
-    )(
-        stem.reshape(pieces, rl, channels), top_lower, top_upper.reshape(pieces, ru, width),
-        seed_lower.reshape(pieces, rl, channels), seed_upper.reshape(pieces, ru, width),
-        gain_lower, gain_upper, *weights,
-    )
-    flat = [r.reshape(-1, r.shape[-1]) for r in results]
-    return flat
 
 
 SLAB = 256
@@ -322,11 +256,6 @@
     mate = lambda other: {"col": high * row + other}
     mirror = {"col": (1 - high) * row + x}
 
-    barrier = pltpu.get_barrier_semaphore()
-    for target in (peer, across, mirror) + toward + tuple(mate(o) for o in mates):
-        pl.semaphore_signal(barrier, inc=1, device_id=target, device_id_type=MESH)
-    pl.semaphore_wait(barrier, 4 + row)
-
     def remote(source, target, send, recv, device):
         return pltpu.make_async_remote_copy(
             src_ref=source, dst_ref=target, send_sem=send, recv_sem=recv,
@@ -339,10 +268,11 @@
             "merge": (folded, dmerged, plan["merge"]), "outer": (lgate, gl, plan["outer"]),
             "inner": (normed, dlh, plan["inner"]), "lift": (ucast, dlift, plan["lift"]),
         }[name]
-        height, width = left.shape[1], right.shape[1]
+        height, width = left.shape[2], right.shape[2]
+        whole = right[...].reshape(-1, width)
         block = height // (4 * depth)
         for top in range(0, height, SLAB):
-            grad = left_outer(left[:, top:top + SLAB], right[...])
+            grad = left_outer(left[:, :, top:top + SLAB].reshape(-1, SLAB), whole)
             count = SLAB // (4 * block)
             z0 = top // (4 * block)
             for slab in range(width // SLAB):
@@ -351,37 +281,37 @@
                 for yb in range(2):
                     part[yb * depth + z0:yb * depth + z0 + count, :, rows, :] = piece[:, yb]
 
-    a1, a2 = (0, plan["outer"], True), (plan["outer"], rows_a - plan["outer"], True)
-    b1 = (rows_a, plan["merge"] - rows_a, False)
-    b2 = (plan["merge"], part.shape[2] - plan["merge"], False)
+    a1, a2 = (0, plan["outer"], True, 0), (plan["outer"], rows_a - plan["outer"], True, 1)
+    b1 = (rows_a, plan["merge"] - rows_a, False, 2)
+    b2 = (plan["merge"], part.shape[2] - plan["merge"], False, 3)
 
     def near_copy(group):
-        start, rows, _ = group
+        start, rows, _, number = group
         return remote(
             part.at[:, 1 - core, pl.ds(start, rows)], near.at[:, pl.ds(start, rows)],
-            near_sem.at[0, start // 16], near_sem.at[1, start // 16], peer,
+            near_sem.at[0, number], near_sem.at[1, number], peer,
         )
 
     def side_copy(group):
-        start, rows, _ = group
+        start, rows, _, number = group
         return remote(
             near.at[pl.ds((1 - y) * depth, depth), pl.ds(start, rows)],
             side.at[:, pl.ds(start - rows_a, rows)],
-            side_sem.at[0, start // 16], side_sem.at[1, start // 16], across,
+            side_sem.at[0, number - 2], side_sem.at[1, number - 2], across,
         )
 
     def flows(group):
-        start, rows, first = group
+        start, rows, first, number = group
         found = []
         for lane in range(2):
             for way in range(2):
                 steps = depth // 2 if way == lane else depth // 2 - 1
                 if first:
-                    found.append((way, lane, steps, start, rows, lane, start))
+                    found.append((way, lane, steps, start, rows, lane, start, number))
                 else:
                     half = rows // 2
                     slot = rows_a + (start - rows_a) // 2
-                    found.append((way, lane, steps, start + lane * half, half, y, slot))
+                    found.append((way, lane, steps, start + lane * half, half, y, slot, number))
         return found
 
     def block_at(flow, step):
@@ -391,24 +321,24 @@
         return (z + depth - steps + step) % depth
 
     def gathered(group, flow, zb):
-        way, lane, steps, start, rows, yb, slot = flow
+        way, lane, steps, start, rows, yb, slot, number = flow
         value = near[yb * depth + zb, start:start + rows] + part[yb * depth + zb, core, start:start + rows]
         if not group[2]:
             value = value + side[zb, start - rows_a:start - rows_a + rows]
         return value
 
     def ring_copy(flow, step):
-        way, lane, steps, start, rows, yb, slot = flow
+        way, lane, steps, start, rows, yb, slot, number = flow
         return remote(
             near.at[yb * depth + block_at(flow, step), pl.ds(start, rows)],
             ring.at[way, lane, step, pl.ds(slot, rows)],
-            ring_sem.at[0, way, lane, step, slot // 16], ring_sem.at[1, way, lane, step, slot // 16],
+            ring_sem.at[0, way, lane, step, number], ring_sem.at[1, way, lane, step, number],
             toward[way],
         )
 
     def ring_step(group, step):
         for flow in flows(group):
-            way, lane, steps, start, rows, yb, slot = flow
+            way, lane, steps, start, rows, yb, slot, number = flow
             if step >= steps:
                 continue
             zb = block_at(flow, step)
@@ -423,7 +353,7 @@
         found = flows(group)
         for lane in range(2):
             pair = [flow for flow in found if flow[1] == lane]
-            way, lane, steps, start, rows, yb, slot = pair[0]
+            way, lane, steps, start, rows, yb, slot, number = pair[0]
             value = gathered(group, pair[0], z)
             for flow in pair:
                 ring_copy(flow, flow[2] - 1).wait_recv()
@@ -431,7 +361,7 @@
             near[yb * depth + z, start:start + rows] = value
 
     def side_open(group):
-        start, rows, _ = group
+        start, rows, _, number = group
 
         def add(zb, carry):
             b = (1 - y) * depth + zb
@@ -441,27 +371,27 @@
         lax.fori_loop(0, depth, add, 0)
         side_copy(group).start()
 
-    a1, a2 = (0, plan["outer"], True), (plan["outer"], rows_a - plan["outer"], True)
-    b1 = (rows_a, plan["merge"] - rows_a, False)
-    b2 = (plan["merge"], part.shape[2] - plan["merge"], False)
-
-    quarter = stem_part.shape[0] // row
+    a1, a2 = (0, plan["outer"], True, 0), (plan["outer"], rows_a - plan["outer"], True, 1)
+    b1 = (rows_a, plan["merge"] - rows_a, False, 2)
+    b2 = (plan["merge"], part.shape[2] - plan["merge"], False, 3)
+
+    quarter = stem_part.shape[1] // row
     half = quarter // 2
     span = lambda index, size: pl.ds(pl.multiple_of(index * size, size), size)
 
     def row_copy(target, slot):
         return remote(
-            stem_part.at[span(target, quarter)], stem_got.at[slot],
+            stem_part.at[:, span(target, quarter)], stem_got.at[slot],
             row_sem.at[0, target], row_sem.at[1, slot], mate(target),
         )
 
     half_copy = remote(
-        stem_half.at[0, span(1 - high, half)], stem_half.at[1, pl.ds(0, half)],
+        stem_half.at[0, :, span(1 - high, half)], stem_half.at[1, :, pl.ds(0, half)],
         half_sem.at[0], half_sem.at[1], mirror,
     )
 
     def back_copy(part_of):
-        ref = stem_full.at[x, span(part_of, half)]
+        ref = stem_full.at[x, :, span(part_of, half)]
         return remote(ref, ref, half_sem.at[2], half_sem.at[3], mirror)
 
     def full_copy(target, slot):
@@ -469,7 +399,7 @@
         return remote(ref, ref, full_sem.at[0, target], full_sem.at[1, slot], mate(target))
 
     def stem_rows():
-        total = stem_part[span(x, quarter), :]
+        total = stem_part[:, span(x, quarter), :]
         for other in mates:
             row_copy(other, other).wait_recv()
             total = total + stem_got[other]
@@ -478,7 +408,9 @@
 
     def stem_mirror():
         half_copy.wait_recv()
-        stem_full[x, span(high, half), :] = stem_half[0, span(high, half), :] + stem_half[1, 0:half]
+        stem_full[x, :, span(high, half), :] = (
+            stem_half[0, :, span(high, half), :] + stem_half[1, :, 0:half]
+        )
         back_copy(high).start()
 
     def stem_spread():
@@ -486,8 +418,6 @@
         for other in mates:
             full_copy(other, x).start()
 
-    for other in mates:
-        row_copy(other, x).start()
     weight_grad("expand")
     near_copy(b1).start()
     weight_grad("reduce")
@@ -505,6 +435,8 @@
     side_open(b2)
     near_copy(a2).wait_recv()
     ring_step(a2, 0)
+    for other in mates:
+        row_copy(other, x).start()
     ring_step(a1, 1)
     ring_step(a2, 1)
     ring_step(a1, 2)
@@ -531,8 +463,15 @@
     ring_step(b2, depth // 2 - 1)
     for other in mates:
         full_copy(other, other).wait_recv()
-    stem_store = pltpu.make_async_copy(stem_full, stem_out, out_sem)
-    stem_store.start()
+    lanes = stem_full.shape[3]
+    stem_stores = [
+        pltpu.make_async_copy(
+            stem_full.at[:, h], stem_out.at[:, :, pl.ds(h * lanes, lanes)], out_sem.at[h]
+        )
+        for h in range(2)
+    ]
+    for store in stem_stores:
+        store.start()
     last_copy.wait_recv()
     packed_out[0:rows_a] = (near[y * depth + z, 0:rows_a] + last[...]) * factor
     ring_end(b1)
@@ -552,14 +491,52 @@
     for other in mates:
         row_copy(other, x).wait_send()
         full_copy(other, x).wait_send()
-    stem_store.wait()
-
-
-def run_scatter(saved, shapes, factor):
+    for store in stem_stores:
+        store.wait()
+
+
+def whole_kernel(pieces, columns, depth, factor, plan, rows_a, *refs):
+    inputs, outs, refs = refs[:13], refs[13:15], refs[15:]
+    tables, load_sem, refs = refs[-7:-1], refs[-1], refs[:-7]
+    loads = [
+        pltpu.make_async_copy(source, table, load_sem.at[i])
+        for i, (source, table) in enumerate(zip(inputs[7:], tables))
+    ]
+    for index in (3, 4, 5, 0, 1, 2):
+        loads[index].start()
+    saved, column_scratch, scatter_scratch = refs[:13], refs[13:27], refs[27:]
+    column, place = lax.axis_index("col"), lax.axis_index("dp")
+    z, y, core = place // 4, (place // 2) % 2, place % 2
+    row = columns // 2
+    x, high = column % row, column // row
+    at = lambda z, y, core: {"dp": z * 4 + y * 2 + core}
+    targets = [at(z, y, 1 - core), at(z, 1 - y, core)]
+    targets += [at((z + 1) % depth, y, core), at((z + depth - 1) % depth, y, core)]
+    targets += [{"col": (1 - high) * row + x}, {"col": columns - 1 - column}]
+    targets += [{"col": high * row + (x + d) % row} for d in range(1, row)]
+    barrier = pltpu.get_barrier_semaphore()
+    for target in targets:
+        pl.semaphore_signal(barrier, inc=1, device_id=target, device_id_type=MESH)
+
+    pl.semaphore_wait(barrier, len(targets))
+    for load in loads:
+        load.wait()
+    column_kernel(pieces, columns, *inputs[:7], *tables, *saved, *column_scratch)
+    scatter_kernel(columns, depth, factor, plan, rows_a, *saved, *outs, *scatter_scratch)
+
+
+def run(stem, top_lower, top_upper, seed_lower, seed_upper, gain_lower, gain_upper, weights, factor):
+    pieces = PIECES
+    lower_rows, channels = stem.shape
+    upper_rows, width = top_upper.shape
+    ru = upper_rows // pieces
+    rl = lower_rows // pieces
+    hidden_up = weights[4].shape[1]
+    hidden_low = weights[1].shape[1]
     devices = lax.axis_size("dp")
     columns = lax.axis_size("col")
     depth = devices // 4
-    blocks = [(rows // devices, cols) for rows, cols in shapes]
+    blocks = [(w.shape[0] // devices, w.shape[1]) for w in weights]
     heights = {
         name: block * (cols // SLAB)
         for name, (block, cols) in zip(("lift", "inner", "outer", "merge", "expand", "reduce"), blocks)
@@ -571,32 +548,53 @@
     rows_a = plan["expand"]
     slots = rows_a + (height - rows_a) // 2
     row = columns // 2
-    stem_part = saved[-1]
-    quarter = (stem_part.shape[0] // row, stem_part.shape[1])
-    full = (row,) + quarter
+    quarter = lower_rows // row
+    lanes = channels // 2
+    full = (row, quarter, channels)
+    kept = lambda rows, cols: pltpu.VMEM((pieces, rows, cols), BF16)
+    low_slot = pltpu.VMEM((pieces, FOLD, ru, channels), F32)
+    up_slot = pltpu.VMEM((pieces, ru, width), F32)
+    half = pltpu.VMEM((2, lower_rows, lanes), F32)
     vmem = pl.BlockSpec(memory_space=pltpu.VMEM)
     away = pl.BlockSpec(memory_space=pl.ANY)
     dma = pltpu.SemaphoreType.DMA
-    packed, stem = pl.pallas_call(
-        functools.partial(scatter_kernel, columns, depth, factor, plan, rows_a),
+    saved = [
+        kept(ru, FOLD * channels), kept(ru, width), kept(ru, hidden_up), kept(ru, width),
+        kept(ru, hidden_up), kept(ru, width), kept(ru, width), kept(ru, channels),
+        kept(rl, channels), kept(rl, hidden_low), kept(rl, channels), kept(rl, hidden_low), half,
+    ]
+    column_scratch = [
+        low_slot, up_slot, low_slot, up_slot, low_slot, up_slot, low_slot, up_slot,
+        pltpu.VMEM((ru, hidden_up), F32), pltpu.VMEM((rl, hidden_low), F32), half,
+        dma((4, pieces)), dma((4, pieces)), dma((2,)),
+    ]
+    scatter_scratch = [
+        pltpu.VMEM((2 * depth, 2, height, SLAB), F32),
+        pltpu.VMEM((2 * depth, height, SLAB), F32),
+        pltpu.VMEM((depth, height - rows_a, SLAB), F32),
+        pltpu.VMEM((rows_a, SLAB), F32),
+        pltpu.VMEM((2, 2, depth // 2, slots, SLAB), F32),
+        pltpu.VMEM((row, 2, quarter, lanes), F32), pltpu.VMEM((2, 2, quarter, lanes), F32),
+        pltpu.VMEM((row, 2, quarter, lanes), F32),
+        dma((2, 4)), dma((2, 2)), dma((2,)), dma((2, 2, 2, depth // 2, 4)),
+        dma((2, row)), dma((4,)), dma((2, row)), dma((2,)),
+    ]
+    tables = [pltpu.VMEM(w.shape, BF16) for w in weights] + [dma((6,))]
+    packed, stem_sum = pl.pallas_call(
+        functools.partial(whole_kernel, pieces, columns, depth, factor, plan, rows_a),
         out_shape=(jax.ShapeDtypeStruct((height, SLAB), F32), jax.ShapeDtypeStruct(full, F32)),
-        in_specs=[vmem] * 13,
+        in_specs=[vmem, away] + [vmem] * 5 + [away] * 6,
         out_specs=(vmem, away),
-        scratch_shapes=[
-            pltpu.VMEM((2 * depth, 2, height, SLAB), F32),
-            pltpu.VMEM((2 * depth, height, SLAB), F32),
-            pltpu.VMEM((depth, height - rows_a, SLAB), F32),
-            pltpu.VMEM((rows_a, SLAB), F32),
-            pltpu.VMEM((2, 2, depth // 2, slots, SLAB), F32),
-            pltpu.VMEM(full, F32), pltpu.VMEM((2,) + quarter, F32), pltpu.VMEM(full, F32),
-            dma((2, 32)), dma((2, 32)), dma((2,)), dma((2, 2, 2, depth // 2, 32)),
-            dma((2, row)), dma((4,)), dma((2, row)), dma,
-        ],
+        scratch_shapes=saved + column_scratch + scatter_scratch + tables,
         compiler_params=pltpu.CompilerParams(
-            collective_id=1, has_side_effects=True, vmem_limit_bytes=VMEM_LIMIT
+            collective_id=0, has_side_effects=True, vmem_limit_bytes=VMEM_LIMIT
         ),
-        name="scatter",
-    )(*saved)
+        name="columns",
+    )(
+        stem.reshape(pieces, rl, channels), top_lower, top_upper.reshape(pieces, ru, width),
+        seed_lower.reshape(pieces, rl, channels), seed_upper.reshape(pieces, ru, width),
+        gain_lower, gain_upper, *weights,
+    )
     names = ("lift", "inner", "outer", "merge", "expand", "reduce")
 
     def finish(packed_ref, stem_ref, *rest):
@@ -616,18 +614,17 @@
         out_specs=tuple([vmem] * 7),
         compiler_params=pltpu.CompilerParams(vmem_limit_bytes=VMEM_LIMIT),
         name="finish",
-    )(packed, stem)
+    )(packed, stem_sum)
 
 
 def shards(stem_input, top_lower, top_upper, seed_lower, seed_upper, gamma_lower, gamma_upper, *weights):
     flat = lambda array: array.reshape(-1, array.shape[-1])
-    weights = [w[0] for w in weights]
-    saved = run_columns(
+    lower_rows = stem_input.shape[0] * stem_input.shape[1]
+    results = run(
         flat(stem_input), flat(top_lower), flat(top_upper), flat(seed_lower), flat(seed_upper),
-        gamma_lower, gamma_upper, weights,
+        gamma_lower, gamma_upper, [w[0] for w in weights],
+        1.0 / math.sqrt(lower_rows * lax.axis_size("dp")),
     )
-    factor = 1.0 / math.sqrt(saved[-1].shape[0] * lax.axis_size("dp"))
-    results = run_scatter(saved, [w.shape for w in weights], factor)
     return tuple(r[None] for r in results[:6]) + (results[6].reshape(stem_input.shape),)
 
 

time: 212 us -> 188 us (0.89)
  Pallas kernels: 211 us -> 187 us
    pallas_call x3 -> x2, Pallas kernels: 211 us -> 187 us  [the longest x1 185 us: run(): pl.pallas_call(functools.partial(whole_kernel, pieces, columns, depth, fa...]
where the time goes in v3:
time: 188 us
  Pallas kernels  187 us (99%)
    pallas_call x1, Pallas kernels, run(): pl.pallas_call(functools.partial(whole_kernel, pieces, columns, depth, fa...  185 us

profile of v3, /device:TPU:1, one launch (start us, length us, event | category | flops | bytes accessed | tf_op | source)
XLA Modules:
  0.0 187.8 jit_solution(6827953878652440685)
XLA Ops:
  0.6 184.7 %columns.1 = (f32[400,256]{1,0:T(8,128)}, f32[4,256,256]{2,1,0:T(8,128)}) custom-call(bf16[16,64,256]{2,1,0:T(8,128)(2,1)} %bitcast.21, f32[1024,256]{1,0:T(8,128)} %bitcast.19, f32[16,16,512]{2,1,0:T(8,128)} %bitcast.22, bf16[16,64,256]{2,1,0:T(8,128)(2,1)} %bitcast.23, bf16[16,16,512]{2,1,0:T(8,128)(2,1)} %bitcast.26, f32[1,256]{1,0:T(1,128)} %refs_5_.1, ...), custom_call_target="tpu_custom_call" | custom-call | tf_op jit(solution)/shard_map/columns/pallas_call | solution.py:583
  185.4 2.5 %finish.1 = (f32[16,256]{1,0:T(8,128)}, f32[8,1024]{1,0:T(8,128)}, f32[32,256]{1,0:T(8,128)}, f32[32,512]{1,0:T(8,128)}, f32[16,2048]{1,0:T(8,128)}, /*index=5*/f32[64,512]{1,0:T(8,128)}, f32[4,256,256]{2,1,0:T(8,128)}) custom-call(f32[400,256]{1,0:T(8,128)} %get-tuple-element.16.packed_ref, f32[4,256,256]{2,1,0:T(8,128)} %get-tuple-element.17.stem_ref), custom_call_target="tpu_custom_call" | custom-call | tf_op jit(solution)/shard_map/finish/pallas_call | solution.py:610

commit v4 on v3

--- a/solution.py
+++ b/solution.py
@@ -48,7 +48,7 @@
 
 
 def column_kernel(
-    pieces, columns,
+    pieces, columns, table_loads,
     stem, top_lower, top_upper, seed_lower, seed_upper, gain_lower, gain_upper,
     lift, inner, outer, merge, expand, reduce,
     folded_out, merged_out, ugate_out, gu_out, duh_out, dmerged_out,
@@ -91,7 +91,7 @@
         return pltpu.make_async_remote_copy(
             src_ref=source.at[p],
             dst_ref=target.at[p],
-            send_sem=send_sem.at[kind, p],
+            send_sem=send_sem.at[kind],
             recv_sem=recv_sem.at[kind, p],
             device_id={"col": column - 1},
             device_id_type=MESH,
@@ -113,6 +113,9 @@
     def _():
         for load in loads:
             load.wait()
+
+    for load in table_loads:
+        load.wait()
 
     spot = lax.broadcasted_iota(jnp.int32, (rl, rl), 0)
     token = lax.broadcasted_iota(jnp.int32, (rl, rl), 1)
@@ -225,12 +228,11 @@
 
     @pl.when(has_next)
     def _():
-        def drain(p, carry):
-            for kind in range(4):
-                copy(kind, p).wait_send()
-            return carry
-
-        lax.fori_loop(0, pieces, drain, 0)
+        for kind, (source, target) in enumerate(streams):
+            pltpu.make_async_remote_copy(
+                src_ref=source, dst_ref=target, send_sem=send_sem.at[kind],
+                recv_sem=recv_sem.at[kind, 0], device_id={"col": column - 1}, device_id_type=MESH,
+            ).wait_send()
 
 
 SLAB = 256
@@ -519,9 +521,7 @@
         pl.semaphore_signal(barrier, inc=1, device_id=target, device_id_type=MESH)
 
     pl.semaphore_wait(barrier, len(targets))
-    for load in loads:
-        load.wait()
-    column_kernel(pieces, columns, *inputs[:7], *tables, *saved, *column_scratch)
+    column_kernel(pieces, columns, loads, *inputs[:7], *tables, *saved, *column_scratch)
     scatter_kernel(columns, depth, factor, plan, rows_a, *saved, *outs, *scatter_scratch)
 
 
@@ -566,7 +566,7 @@
     column_scratch = [
         low_slot, up_slot, low_slot, up_slot, low_slot, up_slot, low_slot, up_slot,
         pltpu.VMEM((ru, hidden_up), F32), pltpu.VMEM((rl, hidden_low), F32), half,
-        dma((4, pieces)), dma((4, pieces)), dma((2,)),
+        dma((4,)), dma((4, pieces)), dma((2,)),
     ]
     scatter_scratch = [
         pltpu.VMEM((2 * depth, 2, height, SLAB), F32),

time: 188 us -> 187 us (level)
  no operation moved by 1% of the time
where the time goes in v4:
time: 187 us
  Pallas kernels  186 us (99%)
    pallas_call x1, Pallas kernels, run(): pl.pallas_call(functools.partial(whole_kernel, pieces, columns, depth, fa...  184 us

profile of v4, /device:TPU:1, one launch (start us, length us, event | category | flops | bytes accessed | tf_op | source)
XLA Modules:
  0.0 186.8 jit_solution(3797057961438971171)
XLA Ops:
  0.6 183.7 %columns.1 = (f32[400,256]{1,0:T(8,128)}, f32[4,256,256]{2,1,0:T(8,128)}) custom-call(bf16[16,64,256]{2,1,0:T(8,128)(2,1)} %bitcast.21, f32[1024,256]{1,0:T(8,128)} %bitcast.19, f32[16,16,512]{2,1,0:T(8,128)} %bitcast.22, bf16[16,64,256]{2,1,0:T(8,128)(2,1)} %bitcast.23, bf16[16,16,512]{2,1,0:T(8,128)(2,1)} %bitcast.26, f32[1,256]{1,0:T(1,128)} %refs_5_.1, ...), custom_call_target="tpu_custom_call" | custom-call | tf_op jit(solution)/shard_map/columns/pallas_call | solution.py:583
  184.3 2.5 %finish.1 = (f32[16,256]{1,0:T(8,128)}, f32[8,1024]{1,0:T(8,128)}, f32[32,256]{1,0:T(8,128)}, f32[32,512]{1,0:T(8,128)}, f32[16,2048]{1,0:T(8,128)}, /*index=5*/f32[64,512]{1,0:T(8,128)}, f32[4,256,256]{2,1,0:T(8,128)}) custom-call(f32[400,256]{1,0:T(8,128)} %get-tuple-element.16.packed_ref, f32[4,256,256]{2,1,0:T(8,128)} %get-tuple-element.17.stem_ref), custom_call_target="tpu_custom_call" | custom-call | tf_op jit(solution)/shard_map/finish/pallas_call | solution.py:610
